TPU v7x, 32 devices: a whole 2x2x4 slice. The times are simulated.
32 devices in a mesh: grp: 2 (over x), src: 8 (over z, y), tgt: 2 (over core).
Axes of the slice: x: 2, y: 2, z: 4, core: 2. Of those that a mesh axis runs over, the one named last changes fastest.
Arguments:
- sources: bfloat16 [2048, 64, 256], P(('grp', 'src', 'tgt')), parts along dimension 0, may hold values from -6 to 6
- warp: bfloat16 [2048], P(('grp', 'src', 'tgt')), parts along dimension 0, may hold values from 0.5 to 2
- interp: bfloat16 [2, 2, 64, 64], replicated, may hold values from -0.75 to 0.75
- omega: float32 [2, 2, 64, 64], replicated, may hold values from -8 to 8
- eval_interp: bfloat16 [64, 64], replicated, may hold values from -0.75 to 0.75
- eval_omega: float32 [64, 64], replicated, may hold values from -8 to 8
Outputs:
- values: float32 [2048, 64, 256], P(('grp', 'src', 'tgt')), parts along dimension 0
There are 2 independent parts, one for each index of `grp`. A program takes and returns all parts, laid end to end along the dimension named above; an argument that names none is the same for every part. Nothing has to cross between parts.
All inputs are finite; a program needn't handle non-finite values.
Results may differ from a plain program's by a relative error of at most 0.012.
The roundings to bfloat16 on the way count: a program that leaves them out, or rounds other values in their place, can miss the bound.
Values may be sent and summed in bfloat16 or wider, within the bound.
No kernel may reach another device: no remote copies, remote signals or barrier semaphores. Data moves between devices by JAX's collectives and lax.ppermute only.
A program may use at most 64 MiB of HBM per device.

v0:
```python
import functools
import math

import jax
import jax.numpy as jnp
from jax import lax
from jax.experimental import pallas as pl
from jax.experimental.pallas import tpu as pltpu
from jax.sharding import PartitionSpec as P

BATCH = 16
GROUP_BITS = 3
HALVES = 2
VMEM_LIMIT = 20 * 1024 * 1024
WARP_ROWS = 16
VMEM = pl.BlockSpec(memory_space=pltpu.VMEM)
ANY = pl.BlockSpec(memory_space=pl.ANY)
HBM = pl.BlockSpec(memory_space=pltpu.HBM)
SINE = (6.28318516, -41.34165503, 81.60100405, -76.54978181, 39.53670223)
LANES = 128


def cosine(turns):
    u = turns - jnp.round(turns)
    z = 0.25 - jnp.abs(u)
    v = z * z
    poly = SINE[-1]
    for coefficient in SINE[-2::-1]:
        poly = poly * v + coefficient
    return z * poly


def tile(gains, turns, scale):
    return (gains * cosine(turns * scale)).astype(jnp.bfloat16)


def product(tiles, state):
    return jnp.dot(tiles, state, preferred_element_type=jnp.float32)


def split_pair(index, bit):
    low = index & ((1 << bit) - 1)
    return ((index >> bit) << (bit + 1)) | low


def pairs_of(count, bit):
    firsts = [split_pair(i, bit) for i in range(count // 2)]
    return [(i, first, first | (1 << bit)) for i, first in enumerate(firsts)]


def multiply(pairs, tiles, load, store):
    for start in range(0, len(pairs), BATCH):
        batch = pairs[start:start + BATCH]
        states = [jnp.concatenate([load(first), load(second)], axis=0) for _, first, second in batch]
        results = [product(tiles(i), x).astype(jnp.bfloat16) for (i, _, _), x in zip(batch, states)]
        for (_, first, second), y in zip(batch, results):
            rank = y.shape[0] // 2
            store(first, y[:rank])
            store(second, y[rank:])


def stack_tables(interp_ref, omega_ref, gains, turns, flips):
    rank = interp_ref.shape[-1]
    for table, out, scale in ((interp_ref, gains, 1.0), (omega_ref, turns, 0.5 / math.pi)):
        for flip in range(flips):
            for row in range(2):
                child = row ^ flip
                for column in range(2):
                    part = table[child, row ^ column].astype(jnp.float32) * scale
                    out[flip, row * rank:(row + 1) * rank, column * rank:(column + 1) * rank] = part


def scale_rows(warp_ref, rows):
    count = rows.shape[0]
    warp = jnp.broadcast_to(warp_ref[...].astype(jnp.float32), (count, count))
    diagonal = lax.broadcasted_iota(jnp.int32, (count, count), 0) == lax.broadcasted_iota(jnp.int32, (count, count), 1)
    column = jnp.sum(jnp.where(diagonal, warp, 0.0), axis=1, keepdims=True)
    rows[...] = jnp.broadcast_to(column, rows.shape)


def local_kernel(groups, group_bits, *refs):
    given, outs, rest = refs[:4], refs[4:4 + groups], refs[4 + groups:]
    warp_ref, interp_ref, omega_ref, state, gains, turns, rows, tiles, sems = rest
    copies = [pltpu.make_async_copy(src, dst, sems.at[i]) for i, (src, dst) in enumerate(zip(given, rest))]
    for copy in copies:
        copy.start()
    for copy in copies[:3]:
        copy.wait()
    stack_tables(interp_ref, omega_ref, gains, turns, 1)
    scale_rows(warp_ref, rows)
    total, rank, width = state.shape
    bits = total.bit_length() - 1
    place = lax.axis_index("src")

    def make_tiles(box):
        for child in range(2):
            half = slice(child * rank, (child + 1) * rank)
            wanted = [level for level in range(bits) if box >> level & 1 == child]
            if wanted:
                before, now = None, cosine(turns[0, half] * (rows[box:box + 1] * 0.25))
                twice = now + now
                for level in range(max(wanted) + 1):
                    if level:
                        before, now = now, twice * now - (1.0 if level == 1 else before)
                    if level in wanted:
                        low = box & ((1 << level) - 1)
                        tiles[level, ((box >> (level + 1)) << level) | low, half] = (gains[0, half] * now).astype(jnp.bfloat16)

    def load(box):
        return state[box]

    def store(box, y):
        state[box] = y

    def level_products(level, pairs):
        multiply(pairs, lambda i: tiles[level, i], load, store)

    size = 1 << group_bits
    for start in range(0, total + size, size):
        for box in range(start, min(start + size, total)):
            make_tiles(box)
        if start == 0:
            copies[3].wait()
        else:
            for level in range(group_bits):
                level_products(level, [p for p in pairs_of(total, level) if start - size <= p[1] < start])
    for level in range(group_bits, bits):
        level_products(level, pairs_of(total, level))

    part = total // groups
    warps = jnp.broadcast_to(warp_ref[...].astype(jnp.float32), (WARP_ROWS, total))
    warps = jnp.concatenate([warps, jnp.zeros((WARP_ROWS, width - total), jnp.float32)], axis=1).astype(jnp.bfloat16)
    for k in range(groups):
        outs[k][:part * rank] = state[pl.ds((place ^ k) * part, part)].reshape(part * rank, width)
        outs[k][part * rank:] = warps


def warp_rows(warps, place, part, rows):
    lanes = lax.broadcasted_iota(jnp.int32, warps.shape, 1)
    for m in range(part):
        column = jnp.sum(jnp.where(lanes == place * part + m, warps, 0.0), axis=1, keepdims=True)
        rows[m] = jnp.broadcast_to(column, rows.shape[1:])


def tiles_kernel(part, first_level, ks, warp_ref, interp_ref, omega_ref, tiles, last_tiles, gains, turns, rows):
    stack_tables(interp_ref, omega_ref, gains, turns, 2)
    rank = interp_ref.shape[-1]
    place, core = lax.axis_index("src"), lax.axis_index("tgt")
    warp_rows(warp_ref[...].astype(jnp.float32), place, part, rows)
    for j, k in enumerate(ks):
        for m in range(part):
            for step in range(tiles.shape[0]):
                side, s = place >> step & 1, k >> step & 1
                half = slice(s * rank, (s + 1) * rank)
                scale = rows[m, j:j + 1] * ((first_level + step + 1) / 4.0)
                tiles[step, k * part + m] = tile(gains[side, half], turns[side, half], scale)
            scale = rows[m, j:j + 1] * ((first_level + tiles.shape[0] + 1) / 4.0)
            last_tiles[k * part + m] = tile(gains[core, :rank], turns[core, :rank], scale)


def remote_kernel(groups, first_m, first_level, tiles, interp_ref, omega_ref, *rest):
    blocks, (out, gains, turns, rows) = rest[:groups], rest[groups:]
    stack_tables(interp_ref, omega_ref, gains, turns, 2)
    count, rank, width = out.shape
    some, part = count // groups, blocks[0].shape[0] // rank
    some_bits = some.bit_length() - 1
    place = lax.axis_index("src")
    warps = blocks[-1][part * rank:, :LANES].astype(jnp.float32)
    warp_rows(warps, place, part, rows)
    for step in range(groups.bit_length() - 1):
        side = place >> step & 1

        def half_tile(i, step=step, side=side):
            k, m = i // some, first_m + i % some
            if k < groups - 1:
                return tiles[step, k * part + m]
            scale = rows[m, :1] * ((first_level + step + 1) / 4.0)
            return tile(gains[side, rank:], turns[side, rank:], scale)

        def load(i, step=step):
            m = first_m + i % some
            return out[i] if step else blocks[i // some][m * rank:(m + 1) * rank]

        def store(i, y):
            out[i] = y

        def tile_of(i, step=step, half_tile=half_tile):
            first = split_pair(i, step + some_bits)
            return jnp.concatenate([half_tile(first), half_tile(first | (1 << (step + some_bits)))], axis=0)

        multiply(pairs_of(count, step + some_bits), tile_of, load, store)


def core_kernel(groups, halves, level, tiles, last_ref, interp_ref, omega_ref, *rest):
    own, other, rest = rest[:halves], rest[halves:2 * halves], rest[2 * halves:]
    outs, (gains, turns, rows) = rest[:groups], rest[groups:]
    stack_tables(interp_ref, omega_ref, gains, turns, 2)
    rank = interp_ref.shape[-1]
    some = own[0].shape[0] // groups
    part = some * halves
    place, core = lax.axis_index("src"), lax.axis_index("tgt")
    warp_rows(last_ref[part * rank:, :LANES].astype(jnp.float32), place, part, rows)
    for k in range(groups):
        for m in range(part):
            i = k * some + m % some
            x = jnp.concatenate([own[m // some][i], other[m // some][i]], axis=0)
            if k < groups - 1:
                tiles_m = tiles[k * part + m]
            else:
                tiles_m = tile(gains[core, :rank], turns[core, :rank], rows[m, :1] * ((level + 1) / 4.0))
            outs[k][m * rank:(m + 1) * rank] = product(tiles_m, x).astype(jnp.bfloat16)


def eval_kernel(ks, warp_ref, interp_ref, omega_ref, *rest):
    blocks = rest[:len(ks)]
    out_hbm, values, rows, sems = rest[-4:]
    rank = interp_ref.shape[-1]
    part = blocks[0].shape[0] // rank
    place = lax.axis_index("src")
    scale_rows(warp_ref, rows)
    gains = interp_ref[...].astype(jnp.float32)
    turns = omega_ref[...] * (0.5 / math.pi)
    gains, turns = jnp.concatenate([gains, gains], axis=1), jnp.concatenate([turns, turns], axis=1)
    left = lax.broadcasted_iota(jnp.int32, (1, 2 * rank), 1) < rank
    copies = []
    for n, k in enumerate(ks):
        group = place ^ k

        def scale_of(m):
            return rows[pl.ds(group * part + m, 1), :]

        for m in range(0, part, 2):
            if m + 1 < part:
                both = tile(gains, turns, jnp.where(left, scale_of(m), scale_of(m + 1)))
                none = jnp.zeros_like(both)
                tiles = jnp.concatenate([jnp.where(left, both, none), jnp.where(left, none, both)], axis=0)
                result = product(tiles, blocks[n][m * rank:(m + 2) * rank])
                values[n, m], values[n, m + 1] = result[:rank], result[rank:]
            else:
                tiles = tile(gains[:, :rank], turns[:, :rank], scale_of(m)[:, :rank])
                values[n, m] = product(tiles, blocks[n][m * rank:(m + 1) * rank])
        copy = pltpu.make_async_copy(values.at[n], out_hbm.at[group], sems.at[n])
        copy.start()
        copies.append(copy)
    for copy in copies:
        copy.wait()


def on_device(sources, warp, interp, omega, eval_interp, eval_omega):
    total, rank, width = sources.shape
    bits = total.bit_length() - 1
    groups = lax.axis_size("src")
    group_bits = groups.bit_length() - 1
    part = total // groups
    halves = min(HALVES, part)
    bf16, f32 = jnp.bfloat16, jnp.float32
    params = pltpu.CompilerParams(vmem_limit_bytes=VMEM_LIMIT)
    warp = warp.reshape(1, total)
    block = jax.ShapeDtypeStruct((part * rank, width), bf16)
    long_block = jax.ShapeDtypeStruct((part * rank + WARP_ROWS, width), bf16)
    both_tables = [pltpu.VMEM((2, 2 * rank, 2 * rank), f32)] * 2
    far, near = list(range(groups // 2, groups)), list(range(1, groups // 2))
    order = [k for pair in zip(far, near) for k in pair] + far[len(near):]

    def cost(steps):
        return pl.CostEstimate(flops=steps, bytes_accessed=steps, transcendentals=0)

    def after(value, done):
        return lax.optimization_barrier((value, done))[0]

    def moved(value, k):
        return lax.ppermute(value, "src", [(i, i ^ k) for i in range(groups)])

    blocks = pl.pallas_call(
        functools.partial(local_kernel, groups, min(GROUP_BITS, bits)),
        out_shape=[long_block] * groups,
        in_specs=[HBM] * 4,
        out_specs=[VMEM] * groups,
        scratch_shapes=[
            pltpu.VMEM(warp.shape, warp.dtype),
            pltpu.VMEM(interp.shape, interp.dtype),
            pltpu.VMEM(omega.shape, omega.dtype),
            pltpu.VMEM((total, rank, width), bf16),
            pltpu.VMEM((1, 2 * rank, 2 * rank), f32),
            pltpu.VMEM((1, 2 * rank, 2 * rank), f32),
            pltpu.VMEM((total, LANES), f32),
            pltpu.VMEM((bits, total // 2, 2 * rank, 2 * rank), bf16),
            pltpu.SemaphoreType.DMA((4,)),
        ],
        compiler_params=params,
        cost_estimate=cost(total // 2 * bits),
        name="local",
    )(warp, interp, omega, sources)
    arrived = {0: blocks[0]}
    for k in order:
        arrived[k] = moved(blocks[k], k)
    known = [0] + order[:-1]
    all_warp = jnp.concatenate([arrived[k][part * rank:part * rank + 1, :total] for k in known], axis=0)
    tiles, last_tiles = pl.pallas_call(
        functools.partial(tiles_kernel, part, bits, known),
        out_shape=[
            jax.ShapeDtypeStruct((group_bits, total - part, rank, 2 * rank), bf16),
            jax.ShapeDtypeStruct((total - part, rank, 2 * rank), bf16),
        ],
        in_specs=[VMEM, VMEM, VMEM],
        out_specs=[VMEM, VMEM],
        scratch_shapes=both_tables + [pltpu.VMEM((part, groups - 1, LANES), f32)],
        compiler_params=params,
        cost_estimate=cost(total // 2 * (group_bits + 1)),
        name="remote_tiles",
    )(all_warp, interp, omega)
    last_rows = pltpu.VMEM((part, WARP_ROWS, LANES), f32)
    last_block = arrived[groups - 1]
    states = []
    for half in range(halves):
        first_m = half * (part // halves)
        by_k = [arrived[k] for k in range(groups)]
        if half:
            by_k[0] = after(by_k[0], states[0])
        states.append(pl.pallas_call(
            functools.partial(remote_kernel, groups, first_m, bits),
            out_shape=jax.ShapeDtypeStruct((total // halves, rank, width), bf16),
            in_specs=[VMEM] * (3 + groups),
            out_specs=VMEM,
            scratch_shapes=both_tables + [last_rows],
            compiler_params=params,
            cost_estimate=cost(total // 2 // halves * group_bits),
            name=f"remote_{half}",
        )(tiles, interp, omega, *by_k))
    others = [lax.ppermute(state, "tgt", [(i, i ^ 1) for i in range(lax.axis_size("tgt"))]) for state in states]
    blocks = pl.pallas_call(
        functools.partial(core_kernel, groups, halves, bits + group_bits),
        out_shape=[block] * groups,
        in_specs=[VMEM] * (4 + 2 * halves),
        out_specs=[VMEM] * groups,
        scratch_shapes=both_tables + [last_rows],
        compiler_params=params,
        cost_estimate=cost(total // 2),
        name="core",
    )(last_tiles, last_block, interp, omega, *states, *others)
    arrived = {0: blocks[0]}
    for k in order:
        arrived[k] = moved(blocks[k], k)
    early = [0] + order[:len(order) // 2]
    values = None
    for name, ks in (("early", early), ("late", [k for k in order if k not in early])):
        operands = [warp, eval_interp, eval_omega] + [arrived[k] for k in ks]
        specs = [VMEM] * len(operands)
        aliases = {}
        if values is not None:
            aliases = {len(operands): 0}
            operands.append(values)
            specs.append(ANY)
        values = pl.pallas_call(
            functools.partial(eval_kernel, ks),
            out_shape=jax.ShapeDtypeStruct((groups, part, rank, width), f32),
            in_specs=specs,
            out_specs=ANY,
            scratch_shapes=[
                pltpu.VMEM((len(ks), part, rank, width), f32),
                pltpu.VMEM((total, LANES), f32),
                pltpu.SemaphoreType.DMA((len(ks),)),
            ],
            input_output_aliases=aliases,
            compiler_params=params,
            cost_estimate=cost(len(ks) * part // 2),
            name=f"eval_{name}",
        )(*operands)
    return values.reshape(total, rank, width)


def solution(mesh):
    in_specs = (P(("grp", "src", "tgt"), None, None), P(("grp", "src", "tgt")), P(), P(), P(), P())
    out_specs = P(("grp", "src", "tgt"), None, None)
    return jax.shard_map(
        on_device, mesh=mesh, in_specs=in_specs, out_specs=out_specs, check_vma=False
    )
```

profile of v0, /device:TPU:16, one launch (start us, length us, event | category | flops | bytes accessed | tf_op | source)
XLA Modules:
  0.0 119.5 jit_solution(10918902984462563670)
XLA Ops:
  0.0 0.9 copy-done
  0.9 1.6 %copy-done.2 = bf16[64,64,256]{2,1,0:T(8,128)(2,1)S(1)} copy-done((bf16[64,64,256]{2,1,0:T(8,128)(2,1)S(1)}, bf16[64,64,256]{2,1,0:T(8,128)(2,1)}, u32[]{:S(2)}) %copy-start.2) | copy-done | bytes 2097176
  2.5 0.8 copy-done.3
  3.3 0.7 copy-done.7
  4.0 6.8 %local.1 = (bf16[528,256]{1,0:T(8,128)(2,1)S(1)}, bf16[528,256]{1,0:T(8,128)(2,1)S(1)}, bf16[528,256]{1,0:T(8,128)(2,1)S(1)}, bf16[528,256]{1,0:T(8,128)(2,1)S(1...) custom-call(bf16[1,64]{1,0:T(2,128)(2,1)S(1)} %bitcast.2, ...), custom_call_target="tpu_custom_call" | custom-call | flops 192 | bytes 192 | tf_op jit(solution)/shard_map/local/pallas_call | solution.py:274
  10.9 1.8 %collective-permute-start.1 = (bf16[528,256]{1,0:T(8,128)(2,1)S(1)}, bf16[528,256]{1,0:T(8,128)(2,1)S(1)}, u32[]{:S(2)}, u32[]{:S(2)}) collective-permute-start(bf16[528,256]{1,0:T(8,128)(2,1)S(1)} %get-tuple-element.26), channel_id=1, source_target_pairs={{0,2},{2,0},{4,6},{6,4},{8,10},{10,8},{12,14},{14,12},{1,3},{3,1},... | collective-permute-start | bytes 811016 | tf_op jit(solution)/shard_map/ppermute | solution.py:272
  12.7 2.5 %collective-permute-start.2 = (bf16[528,256]{1,0:T(8,128)(2,1)S(1)}, bf16[528,256]{1,0:T(8,128)(2,1)S(1)}, u32[]{:S(2)}, u32[]{:S(2)}) collective-permute-start(bf16[528,256]{1,0:T(8,128)(2,1)S(1)} %get-tuple-element.27), channel_id=1, source_target_pairs={{0,10},{2,8},{4,14},{6,12},{8,2},{10,0},{12,6},{14,4},{1,11},{3,9}... | collective-permute-start | bytes 811016 | tf_op jit(solution)/shard_map/ppermute | solution.py:272
  15.3 1.6 %collective-permute-start.3 = (bf16[528,256]{1,0:T(8,128)(2,1)S(1)}, bf16[528,256]{1,0:T(8,128)(2,1)S(1)}, u32[]{:S(2)}, u32[]{:S(2)}) collective-permute-start(bf16[528,256]{1,0:T(8,128)(2,1)S(1)} %get-tuple-element.28), channel_id=1, source_target_pairs={{0,4},{2,6},{4,0},{6,2},{8,12},{10,14},{12,8},{14,10},{1,5},{3,7},... | collective-permute-start | bytes 811016 | tf_op jit(solution)/shard_map/ppermute | solution.py:272
  16.8 12.8 %collective-permute-done.rest_4_ = bf16[528,256]{1,0:T(8,128)(2,1)S(1)} collective-permute-done((bf16[528,256]{1,0:T(8,128)(2,1)S(1)}, bf16[528,256]{1,0:T(8,128)(2,1)S(1)}, u32[]{:S(2)}, u32[]{:S(2)}) %collective-permute-start) | collective-permute-done | bytes 270368 | tf_op jit(solution)/shard_map/ppermute | solution.py:272
  29.6 5.7 %collective-permute-start.5 = (bf16[528,256]{1,0:T(8,128)(2,1)S(1)}, bf16[528,256]{1,0:T(8,128)(2,1)S(1)}, u32[]{:S(2)}, u32[]{:S(2)}) collective-permute-start(bf16[528,256]{1,0:T(8,128)(2,1)S(1)} %get-tuple-element.30), channel_id=1, source_target_pairs={{0,6},{2,4},{4,2},{6,0},{8,14},{10,12},{12,10},{14,8},{1,7},{3,5},... | collective-permute-start | bytes 811016 | tf_op jit(solution)/shard_map/ppermute | solution.py:272
  35.3 5.9 %collective-permute-done.2.rest_5_ = bf16[528,256]{1,0:T(8,128)(2,1)S(1)} collective-permute-done((bf16[528,256]{1,0:T(8,128)(2,1)S(1)}, bf16[528,256]{1,0:T(8,128)(2,1)S(1)}, u32[]{:S(2)}, u32[]{:S(2)}) %collective-permute-start.2) | collective-permute-done | bytes 270368 | tf_op jit(solution)/shard_map/ppermute | solution.py:272
  41.2 13.7 %collective-permute-done.4.rest_6_ = bf16[528,256]{1,0:T(8,128)(2,1)S(1)} collective-permute-done((bf16[528,256]{1,0:T(8,128)(2,1)S(1)}, bf16[528,256]{1,0:T(8,128)(2,1)S(1)}, u32[]{:S(2)}, u32[]{:S(2)}) %collective-permute-start.4) | collective-permute-done | bytes 270368 | tf_op jit(solution)/shard_map/ppermute | solution.py:272
  54.9 0.9 copy-done.1
  55.8 0.8 copy-done.4
  56.7 4.2 %remote_tiles.1 = (bf16[3,56,64,128]{3,2,1,0:T(8,128)(2,1)S(1)}, bf16[56,64,128]{2,1,0:T(8,128)(2,1)S(1)}) custom-call(bf16[7,64]{1,0:T(8,128)(2,1)S(1)} %concatenate.3.warp_ref, bf16[2,2,64,64]{3,2,1,0:T(8,128)(2,1)S(1)} %copy-done.4, f32[2,2,64,64]{3,2,1,0:T(8,128)S(1)} %copy-done.1), custom_call_target="tpu_custom_call" | custom-call | flops 128 | bytes 128 | tf_op jit(solution)/shard_map/remote_tiles/pallas_call | solution.py:299
  60.9 0.6 collective-permute-done.6.rest_7_.last_ref
  61.5 1.0 remote_0.1.rest_0_
  62.5 1.2 %remote_1.1.rest_1_ = bf16[32,64,256]{2,1,0:T(8,128)(2,1)S(1)} custom-call(bf16[3,56,64,128]{3,2,1,0:T(8,128)(2,1)S(1)} %get-tuple-element.33.tiles, bf16[2,2,64,64]{3,2,1,0:T(8,128)(2,1)S(1)} %copy-done.4, f32[2,2,64,64]{3,2,1,0:T(8,128)S(1)} %copy-done.1, bf16[528,256]{1,0:T(8,128)(2,1)S(1)} %get-tuple-element.34.rest_0_, ...), custom_call_target="tpu_custom_call" | custom-call | flops 48 | bytes 48 | tf_op jit(solution)/shard_map/remote_1/pallas_call | solution.py:320
  64.4 2.1 %collective-permute-done.8.rest_3_ = bf16[32,64,256]{2,1,0:T(8,128)(2,1)S(1)} collective-permute-done((bf16[32,64,256]{2,1,0:T(8,128)(2,1)S(1)}, bf16[32,64,256]{2,1,0:T(8,128)(2,1)S(1)}, u32[]{:S(2)}, u32[]{:S(2)}) %collective-permute-start.8) | collective-permute-done | bytes 1048608 | tf_op jit(solution)/shard_map/ppermute | solution.py:330
  66.5 1.5 %collective-permute-done.7.rest_2_ = bf16[32,64,256]{2,1,0:T(8,128)(2,1)S(1)} collective-permute-done((bf16[32,64,256]{2,1,0:T(8,128)(2,1)S(1)}, bf16[32,64,256]{2,1,0:T(8,128)(2,1)S(1)}, u32[]{:S(2)}, u32[]{:S(2)}) %collective-permute-start.7) | collective-permute-done | bytes 1048608 | tf_op jit(solution)/shard_map/ppermute | solution.py:330
  68.0 0.8 core.1
  68.8 0.6 collective-permute-start.13
  69.9 1.8 %collective-permute-start.9 = (bf16[512,256]{1,0:T(8,128)(2,1)S(1)}, bf16[512,256]{1,0:T(8,128)(2,1)S(1)}, u32[]{:S(2)}, u32[]{:S(2)}) collective-permute-start(bf16[512,256]{1,0:T(8,128)(2,1)S(1)} %get-tuple-element.35), channel_id=1, source_target_pairs={{0,4},{2,6},{4,0},{6,2},{8,12},{10,14},{12,8},{14,10},{1,5},{3,7},... | collective-permute-start | bytes 786440 | tf_op jit(solution)/shard_map/ppermute | solution.py:272
  71.7 3.2 %collective-permute-start.15 = (bf16[512,256]{1,0:T(8,128)(2,1)S(1)}, bf16[512,256]{1,0:T(8,128)(2,1)S(1)}, u32[]{:S(2)}, u32[]{:S(2)}) collective-permute-start(bf16[512,256]{1,0:T(8,128)(2,1)S(1)} %get-tuple-element.42), channel_id=1, source_target_pairs={{0,10},{2,8},{4,14},{6,12},{8,2},{10,0},{12,6},{14,4},{1,11},{3,9}... | collective-permute-start | bytes 786440 | tf_op jit(solution)/shard_map/ppermute | solution.py:272
  74.9 6.8 %collective-permute-done.13.rest_1_ = bf16[512,256]{1,0:T(8,128)(2,1)S(1)} collective-permute-done((bf16[512,256]{1,0:T(8,128)(2,1)S(1)}, bf16[512,256]{1,0:T(8,128)(2,1)S(1)}, u32[]{:S(2)}, u32[]{:S(2)}) %collective-permute-start.13) | collective-permute-done | bytes 262176 | tf_op jit(solution)/shard_map/ppermute | solution.py:272
  81.7 4.8 %collective-permute-start.11 = (bf16[512,256]{1,0:T(8,128)(2,1)S(1)}, bf16[512,256]{1,0:T(8,128)(2,1)S(1)}, u32[]{:S(2)}, u32[]{:S(2)}) collective-permute-start(bf16[512,256]{1,0:T(8,128)(2,1)S(1)} %get-tuple-element.37), channel_id=1, source_target_pairs={{0,6},{2,4},{4,2},{6,0},{8,14},{10,12},{12,10},{14,8},{1,7},{3,5},... | collective-permute-start | bytes 786440 | tf_op jit(solution)/shard_map/ppermute | solution.py:272
  86.5 0.5 collective-permute-start.12
  87.0 11.5 %collective-permute-done.15.rest_3_ = bf16[512,256]{1,0:T(8,128)(2,1)S(1)} collective-permute-done((bf16[512,256]{1,0:T(8,128)(2,1)S(1)}, bf16[512,256]{1,0:T(8,128)(2,1)S(1)}, u32[]{:S(2)}, u32[]{:S(2)}) %collective-permute-start.15) | collective-permute-done | bytes 262176 | tf_op jit(solution)/shard_map/ppermute | solution.py:272
  98.6 1.7 %eval_early.1.rest_4_ = f32[8,8,64,256]{3,2,1,0:T(8,128)} custom-call(bf16[1,64]{1,0:T(2,128)(2,1)S(1)} %bitcast.3, bf16[64,64]{1,0:T(8,128)(2,1)S(1)} %copy-done.6, f32[64,64]{1,0:T(8,128)S(1)} %copy-done.5, bf16[512,256]{1,0:T(8,128)(2,1)S(1)} %get-tuple-element.39.rest_0_, bf16[512,256]{1,0:T(8,128)(2,1)S(1)} %collective-permute-done.13.rest_1_, ...), custom_call_target="tpu_custom_call" | custom-call | flops 16 | bytes 16 | tf_op jit(solution)/shard_map/eval_early/pallas_call | solution.py:354
  100.3 11.7 %collective-permute-done.10.rest_1_ = bf16[512,256]{1,0:T(8,128)(2,1)S(1)} collective-permute-done((bf16[512,256]{1,0:T(8,128)(2,1)S(1)}, bf16[512,256]{1,0:T(8,128)(2,1)S(1)}, u32[]{:S(2)}, u32[]{:S(2)}) %collective-permute-start.10) | collective-permute-done | bytes 262176 | tf_op jit(solution)/shard_map/ppermute | solution.py:272
  111.9 5.7 %collective-permute-done.12.rest_3_ = bf16[512,256]{1,0:T(8,128)(2,1)S(1)} collective-permute-done((bf16[512,256]{1,0:T(8,128)(2,1)S(1)}, bf16[512,256]{1,0:T(8,128)(2,1)S(1)}, u32[]{:S(2)}, u32[]{:S(2)}) %collective-permute-start.12) | collective-permute-done | bytes 262176 | tf_op jit(solution)/shard_map/ppermute | solution.py:272
  117.7 1.7 %eval_late.1 = f32[8,8,64,256]{3,2,1,0:T(8,128)} custom-call(bf16[1,64]{1,0:T(2,128)(2,1)S(1)} %bitcast.4, bf16[64,64]{1,0:T(8,128)(2,1)S(1)} %copy-done.6, f32[64,64]{1,0:T(8,128)S(1)} %copy-done.5, bf16[512,256]{1,0:T(8,128)(2,1)S(1)} %collective-permute-done.9.rest_0_, ...), custom_call_target="tpu_custom_call", output_to_operand_aliasing={{}: (7, {})} | custom-call | flops 16 | bytes 16 | tf_op jit(solution)/shard_map/eval_late/pallas_call | solution.py:354
  (33 shorter events, 1.2 us)
Async XLA Ops:
  0.0 0.9 copy-start
  0.9 1.6 %copy-start.2 = (bf16[64,64,256]{2,1,0:T(8,128)(2,1)S(1)}, bf16[64,64,256]{2,1,0:T(8,128)(2,1)}, u32[]{:S(2)}) copy-start(bf16[64,64,256]{2,1,0:T(8,128)(2,1)} %refs_3_.1) | copy-start | bytes 6291460
  2.5 0.8 copy-start.3
  3.3 0.7 copy-start.7
  10.8 18.8 %collective-permute-start = (bf16[528,256]{1,0:T(8,128)(2,1)S(1)}, bf16[528,256]{1,0:T(8,128)(2,1)S(1)}, u32[]{:S(2)}, u32[]{:S(2)}) collective-permute-start(bf16[528,256]{1,0:T(8,128)(2,1)S(1)} %get-tuple-element.25), channel_id=1, source_target_pairs={{0,8},{2,10},{4,12},{6,14},{8,0},{10,2},{12,4},{14,6},{1,9},{3,11}... | collective-permute-start | bytes 811016 | tf_op jit(solution)/shard_map/ppermute | solution.py:272
  10.9 24.4 %collective-permute-start.1 = (bf16[528,256]{1,0:T(8,128)(2,1)S(1)}, bf16[528,256]{1,0:T(8,128)(2,1)S(1)}, u32[]{:S(2)}, u32[]{:S(2)}) collective-permute-start(bf16[528,256]{1,0:T(8,128)(2,1)S(1)} %get-tuple-element.26), channel_id=1, source_target_pairs={{0,2},{2,0},{4,6},{6,4},{8,10},{10,8},{12,14},{14,12},{1,3},{3,1},... | collective-permute-start | bytes 811016 | tf_op jit(solution)/shard_map/ppermute | solution.py:272
  12.7 28.5 %collective-permute-start.2 = (bf16[528,256]{1,0:T(8,128)(2,1)S(1)}, bf16[528,256]{1,0:T(8,128)(2,1)S(1)}, u32[]{:S(2)}, u32[]{:S(2)}) collective-permute-start(bf16[528,256]{1,0:T(8,128)(2,1)S(1)} %get-tuple-element.27), channel_id=1, source_target_pairs={{0,10},{2,8},{4,14},{6,12},{8,2},{10,0},{12,6},{14,4},{1,11},{3,9}... | collective-permute-start | bytes 811016 | tf_op jit(solution)/shard_map/ppermute | solution.py:272
  15.3 25.9 %collective-permute-start.3 = (bf16[528,256]{1,0:T(8,128)(2,1)S(1)}, bf16[528,256]{1,0:T(8,128)(2,1)S(1)}, u32[]{:S(2)}, u32[]{:S(2)}) collective-permute-start(bf16[528,256]{1,0:T(8,128)(2,1)S(1)} %get-tuple-element.28), channel_id=1, source_target_pairs={{0,4},{2,6},{4,0},{6,2},{8,12},{10,14},{12,8},{14,10},{1,5},{3,7},... | collective-permute-start | bytes 811016 | tf_op jit(solution)/shard_map/ppermute | solution.py:272
  16.8 38.1 %collective-permute-start.4 = (bf16[528,256]{1,0:T(8,128)(2,1)S(1)}, bf16[528,256]{1,0:T(8,128)(2,1)S(1)}, u32[]{:S(2)}, u32[]{:S(2)}) collective-permute-start(bf16[528,256]{1,0:T(8,128)(2,1)S(1)} %get-tuple-element.29), channel_id=1, source_target_pairs={{0,12},{2,14},{4,8},{6,10},{8,4},{10,6},{12,0},{14,2},{1,13},{3,15... | collective-permute-start | bytes 811016 | tf_op jit(solution)/shard_map/ppermute | solution.py:272
  29.6 25.3 %collective-permute-start.5 = (bf16[528,256]{1,0:T(8,128)(2,1)S(1)}, bf16[528,256]{1,0:T(8,128)(2,1)S(1)}, u32[]{:S(2)}, u32[]{:S(2)}) collective-permute-start(bf16[528,256]{1,0:T(8,128)(2,1)S(1)} %get-tuple-element.30), channel_id=1, source_target_pairs={{0,6},{2,4},{4,2},{6,0},{8,14},{10,12},{12,10},{14,8},{1,7},{3,5},... | collective-permute-start | bytes 811016 | tf_op jit(solution)/shard_map/ppermute | solution.py:272
  35.2 26.3 %collective-permute-start.6 = (bf16[528,256]{1,0:T(8,128)(2,1)S(1)}, bf16[528,256]{1,0:T(8,128)(2,1)S(1)}, u32[]{:S(2)}, u32[]{:S(2)}) collective-permute-start(bf16[528,256]{1,0:T(8,128)(2,1)S(1)} %get-tuple-element.32), channel_id=1, source_target_pairs={{0,14},{2,12},{4,10},{6,8},{8,6},{10,4},{12,2},{14,0},{1,15},{3,13... | collective-permute-start | bytes 811016 | tf_op jit(solution)/shard_map/ppermute | solution.py:272
  54.9 0.9 copy-start.1
  55.8 0.8 copy-start.4
  63.8 34.8 %copy-start.5 = (f32[64,64]{1,0:T(8,128)S(1)}, f32[64,64]{1,0:T(8,128)}, u32[]{:S(2)}) copy-start(f32[64,64]{1,0:T(8,128)} %omega_ref.11) | copy-start | bytes 49156
  63.8 34.8 %copy-start.6 = (bf16[64,64]{1,0:T(8,128)(2,1)S(1)}, bf16[64,64]{1,0:T(8,128)(2,1)}, u32[]{:S(2)}) copy-start(bf16[64,64]{1,0:T(8,128)(2,1)} %interp_ref.11) | copy-start | bytes 24580
  63.8 34.8 %copy-start.8 = (bf16[64]{0:T(256)(128)(2,1)S(1)}, bf16[64]{0:T(256)(128)(2,1)}, u32[]{:S(2)}) copy-start(bf16[64]{0:T(256)(128)(2,1)} %param.7) | copy-start | bytes 388
  63.8 2.7 %collective-permute-start.8 = (bf16[32,64,256]{2,1,0:T(8,128)(2,1)S(1)}, bf16[32,64,256]{2,1,0:T(8,128)(2,1)S(1)}, u32[]{:S(2)}, u32[]{:S(2)}) collective-permute-start(bf16[32,64,256]{2,1,0:T(8,128)(2,1)S(1)} %remote_1.1.rest_1_), channel_id=1, source_target_pairs={{0,1},{1,0},{2,3},{3,2},{4,5},{5,4},{6,7},{7,6},{8,9},{9,8},{10,11... | collective-permute-start | bytes 3145736 | tf_op jit(solution)/shard_map/ppermute | solution.py:330
  63.9 4.1 %collective-permute-start.7 = (bf16[32,64,256]{2,1,0:T(8,128)(2,1)S(1)}, bf16[32,64,256]{2,1,0:T(8,128)(2,1)S(1)}, u32[]{:S(2)}, u32[]{:S(2)}) collective-permute-start(bf16[32,64,256]{2,1,0:T(8,128)(2,1)S(1)} %remote_0.1.rest_0_), channel_id=1, source_target_pairs={{0,1},{1,0},{2,3},{3,2},{4,5},{5,4},{6,7},{7,6},{8,9},{9,8},{10,11... | collective-permute-start | bytes 3145736 | tf_op jit(solution)/shard_map/ppermute | solution.py:330
  68.8 12.9 %collective-permute-start.13 = (bf16[512,256]{1,0:T(8,128)(2,1)S(1)}, bf16[512,256]{1,0:T(8,128)(2,1)S(1)}, u32[]{:S(2)}, u32[]{:S(2)}) collective-permute-start(bf16[512,256]{1,0:T(8,128)(2,1)S(1)} %get-tuple-element.40), channel_id=1, source_target_pairs={{0,8},{2,10},{4,12},{6,14},{8,0},{10,2},{12,4},{14,6},{1,9},{3,11}... | collective-permute-start | bytes 786440 | tf_op jit(solution)/shard_map/ppermute | solution.py:272
  69.4 17.1 %collective-permute-start.14 = (bf16[512,256]{1,0:T(8,128)(2,1)S(1)}, bf16[512,256]{1,0:T(8,128)(2,1)S(1)}, u32[]{:S(2)}, u32[]{:S(2)}) collective-permute-start(bf16[512,256]{1,0:T(8,128)(2,1)S(1)} %get-tuple-element.41), channel_id=1, source_target_pairs={{0,2},{2,0},{4,6},{6,4},{8,10},{10,8},{12,14},{14,12},{1,3},{3,1},... | collective-permute-start | bytes 786440 | tf_op jit(solution)/shard_map/ppermute | solution.py:272
  69.9 30.4 %collective-permute-start.9 = (bf16[512,256]{1,0:T(8,128)(2,1)S(1)}, bf16[512,256]{1,0:T(8,128)(2,1)S(1)}, u32[]{:S(2)}, u32[]{:S(2)}) collective-permute-start(bf16[512,256]{1,0:T(8,128)(2,1)S(1)} %get-tuple-element.35), channel_id=1, source_target_pairs={{0,4},{2,6},{4,0},{6,2},{8,12},{10,14},{12,8},{14,10},{1,5},{3,7},... | collective-permute-start | bytes 786440 | tf_op jit(solution)/shard_map/ppermute | solution.py:272
  71.7 26.8 %collective-permute-start.15 = (bf16[512,256]{1,0:T(8,128)(2,1)S(1)}, bf16[512,256]{1,0:T(8,128)(2,1)S(1)}, u32[]{:S(2)}, u32[]{:S(2)}) collective-permute-start(bf16[512,256]{1,0:T(8,128)(2,1)S(1)} %get-tuple-element.42), channel_id=1, source_target_pairs={{0,10},{2,8},{4,14},{6,12},{8,2},{10,0},{12,6},{14,4},{1,11},{3,9}... | collective-permute-start | bytes 786440 | tf_op jit(solution)/shard_map/ppermute | solution.py:272
  74.9 37.0 %collective-permute-start.10 = (bf16[512,256]{1,0:T(8,128)(2,1)S(1)}, bf16[512,256]{1,0:T(8,128)(2,1)S(1)}, u32[]{:S(2)}, u32[]{:S(2)}) collective-permute-start(bf16[512,256]{1,0:T(8,128)(2,1)S(1)} %get-tuple-element.36), channel_id=1, source_target_pairs={{0,12},{2,14},{4,8},{6,10},{8,4},{10,6},{12,0},{14,2},{1,13},{3,15... | collective-permute-start | bytes 786440 | tf_op jit(solution)/shard_map/ppermute | solution.py:272
  81.7 30.2 %collective-permute-start.11 = (bf16[512,256]{1,0:T(8,128)(2,1)S(1)}, bf16[512,256]{1,0:T(8,128)(2,1)S(1)}, u32[]{:S(2)}, u32[]{:S(2)}) collective-permute-start(bf16[512,256]{1,0:T(8,128)(2,1)S(1)} %get-tuple-element.37), channel_id=1, source_target_pairs={{0,6},{2,4},{4,2},{6,0},{8,14},{10,12},{12,10},{14,8},{1,7},{3,5},... | collective-permute-start | bytes 786440 | tf_op jit(solution)/shard_map/ppermute | solution.py:272
  86.5 31.2 %collective-permute-start.12 = (bf16[512,256]{1,0:T(8,128)(2,1)S(1)}, bf16[512,256]{1,0:T(8,128)(2,1)S(1)}, u32[]{:S(2)}, u32[]{:S(2)}) collective-permute-start(bf16[512,256]{1,0:T(8,128)(2,1)S(1)} %get-tuple-element.38), channel_id=1, source_target_pairs={{0,14},{2,12},{4,10},{6,8},{8,6},{10,4},{12,2},{14,0},{1,15},{3,13... | collective-permute-start | bytes 786440 | tf_op jit(solution)/shard_map/ppermute | solution.py:272
where the time goes:
time: 120 us
  waiting for transfers between devices  72.3 us (60%)
  starting transfers between devices  23.7 us (20%)
  Pallas kernels  17.4 us (14%)
  local copies, waits for them, and re-layouts  5.79 us (5%)
    ppermute x14, waiting for transfers between devices, moved(): return lax.ppermute(value, 'src', [(i, i ^ k) for i in range(groups)])  68.7 us
    ppermute x14, starting transfers between devices, moved(): return lax.ppermute(value, 'src', [(i, i ^ k) for i in range(groups)])  23.1 us
    pallas_call x1, Pallas kernels, on_device(): pl.pallas_call(functools.partial(local_kernel, groups, min(GROUP_BITS, bi...  6.8 us
    unnamed x18, local copies, waits for them, and re-layouts  5.75 us
    pallas_call x1, Pallas kernels, on_device(): pl.pallas_call(functools.partial(tiles_kernel, part, bits, known), out_sh...  4.24 us
    ppermute x2, waiting for transfers between devices, on_device(): lax.ppermute(state, 'tgt', [(i, i ^ 1) for i in range(lax.axis_size('tgt'...  3.65 us
    pallas_call x2, Pallas kernels, on_device(): pl.pallas_call(functools.partial(eval_kernel, ks), out_shape=jax.ShapeDty...  3.36 us
  transfers between devices with their start and end apart: 16, of which 10 were waited for; matrix products, arithmetic and copies ran while one was open for 0% of the time, Pallas kernels for 5%

commit v1 on v0

--- a/solution.py
+++ b/solution.py
@@ -8,10 +8,12 @@
 from jax.experimental.pallas import tpu as pltpu
 from jax.sharding import PartitionSpec as P
 
+KNOWN = 4
 BATCH = 16
 GROUP_BITS = 3
 HALVES = 2
 VMEM_LIMIT = 20 * 1024 * 1024
+LOCAL_VMEM_LIMIT = 60 * 1024 * 1024
 WARP_ROWS = 16
 VMEM = pl.BlockSpec(memory_space=pltpu.VMEM)
 ANY = pl.BlockSpec(memory_space=pl.ANY)
@@ -78,8 +80,8 @@
     rows[...] = jnp.broadcast_to(column, rows.shape)
 
 
-def local_kernel(groups, group_bits, *refs):
-    given, outs, rest = refs[:4], refs[4:4 + groups], refs[4 + groups:]
+def local_kernel(groups, halves, group_bits, *refs):
+    given, outs, rest = refs[:4], refs[4:4 + halves * groups], refs[4 + halves * groups:]
     warp_ref, interp_ref, omega_ref, state, gains, turns, rows, tiles, sems = rest
     copies = [pltpu.make_async_copy(src, dst, sems.at[i]) for i, (src, dst) in enumerate(zip(given, rest))]
     for copy in copies:
@@ -130,9 +132,13 @@
     part = total // groups
     warps = jnp.broadcast_to(warp_ref[...].astype(jnp.float32), (WARP_ROWS, total))
     warps = jnp.concatenate([warps, jnp.zeros((WARP_ROWS, width - total), jnp.float32)], axis=1).astype(jnp.bfloat16)
+    some = part // halves
     for k in range(groups):
-        outs[k][:part * rank] = state[pl.ds((place ^ k) * part, part)].reshape(part * rank, width)
-        outs[k][part * rank:] = warps
+        for half in range(halves):
+            out = outs[half * groups + k]
+            out[:some * rank] = state[pl.ds((place ^ k) * part + half * some, some)].reshape(some * rank, width)
+            if half == 0:
+                out[some * rank:] = warps
 
 
 def warp_rows(warps, place, part, rows):
@@ -153,32 +159,34 @@
                 side, s = place >> step & 1, k >> step & 1
                 half = slice(s * rank, (s + 1) * rank)
                 scale = rows[m, j:j + 1] * ((first_level + step + 1) / 4.0)
-                tiles[step, k * part + m] = tile(gains[side, half], turns[side, half], scale)
+                tiles[step, j * part + m] = tile(gains[side, half], turns[side, half], scale)
             scale = rows[m, j:j + 1] * ((first_level + tiles.shape[0] + 1) / 4.0)
-            last_tiles[k * part + m] = tile(gains[core, :rank], turns[core, :rank], scale)
-
-
-def remote_kernel(groups, first_m, first_level, tiles, interp_ref, omega_ref, *rest):
-    blocks, (out, gains, turns, rows) = rest[:groups], rest[groups:]
+            last_tiles[j * part + m] = tile(gains[core, :rank], turns[core, :rank], scale)
+
+
+def remote_kernel(groups, first_m, part, first_level, known, tiles, interp_ref, omega_ref, *rest):
+    unknown = [k for k in range(groups) if k not in known]
+    blocks, late, (out, gains, turns, rows) = rest[:groups], rest[groups:groups + len(unknown)], rest[groups + len(unknown):]
     stack_tables(interp_ref, omega_ref, gains, turns, 2)
     count, rank, width = out.shape
-    some, part = count // groups, blocks[0].shape[0] // rank
+    some = count // groups
     some_bits = some.bit_length() - 1
     place = lax.axis_index("src")
-    warps = blocks[-1][part * rank:, :LANES].astype(jnp.float32)
-    warp_rows(warps, place, part, rows)
+    for j, ref in enumerate(late):
+        warp_rows(ref[ref.shape[0] - WARP_ROWS:, :LANES].astype(jnp.float32), place, part, rows.at[j])
     for step in range(groups.bit_length() - 1):
         side = place >> step & 1
 
         def half_tile(i, step=step, side=side):
             k, m = i // some, first_m + i % some
-            if k < groups - 1:
-                return tiles[step, k * part + m]
-            scale = rows[m, :1] * ((first_level + step + 1) / 4.0)
-            return tile(gains[side, rank:], turns[side, rank:], scale)
+            if k in known:
+                return tiles[step, known.index(k) * part + m]
+            scale = rows[unknown.index(k), m, :1] * ((first_level + step + 1) / 4.0)
+            half = slice((k >> step & 1) * rank, ((k >> step & 1) + 1) * rank)
+            return tile(gains[side, half], turns[side, half], scale)
 
         def load(i, step=step):
-            m = first_m + i % some
+            m = i % some
             return out[i] if step else blocks[i // some][m * rank:(m + 1) * rank]
 
         def store(i, y):
@@ -191,31 +199,32 @@
         multiply(pairs_of(count, step + some_bits), tile_of, load, store)
 
 
-def core_kernel(groups, halves, level, tiles, last_ref, interp_ref, omega_ref, *rest):
-    own, other, rest = rest[:halves], rest[halves:2 * halves], rest[2 * halves:]
+def core_kernel(groups, first_m, part, level, known, tiles, interp_ref, omega_ref, own, other, *rest):
+    unknown = [k for k in range(groups) if k not in known]
+    late, rest = rest[:len(unknown)], rest[len(unknown):]
     outs, (gains, turns, rows) = rest[:groups], rest[groups:]
     stack_tables(interp_ref, omega_ref, gains, turns, 2)
     rank = interp_ref.shape[-1]
-    some = own[0].shape[0] // groups
-    part = some * halves
+    some = own.shape[0] // groups
     place, core = lax.axis_index("src"), lax.axis_index("tgt")
-    warp_rows(last_ref[part * rank:, :LANES].astype(jnp.float32), place, part, rows)
+    for j, ref in enumerate(late):
+        warp_rows(ref[ref.shape[0] - WARP_ROWS:, :LANES].astype(jnp.float32), place, part, rows.at[j])
     for k in range(groups):
-        for m in range(part):
-            i = k * some + m % some
-            x = jnp.concatenate([own[m // some][i], other[m // some][i]], axis=0)
-            if k < groups - 1:
-                tiles_m = tiles[k * part + m]
+        for m in range(some):
+            x = jnp.concatenate([own[k * some + m], other[k * some + m]], axis=0)
+            if k in known:
+                tiles_m = tiles[known.index(k) * part + first_m + m]
             else:
-                tiles_m = tile(gains[core, :rank], turns[core, :rank], rows[m, :1] * ((level + 1) / 4.0))
+                scale = rows[unknown.index(k), first_m + m, :1] * ((level + 1) / 4.0)
+                tiles_m = tile(gains[core, :rank], turns[core, :rank], scale)
             outs[k][m * rank:(m + 1) * rank] = product(tiles_m, x).astype(jnp.bfloat16)
 
 
-def eval_kernel(ks, warp_ref, interp_ref, omega_ref, *rest):
-    blocks = rest[:len(ks)]
+def eval_kernel(part, items, warp_ref, interp_ref, omega_ref, *rest):
+    blocks = rest[:len(items)]
     out_hbm, values, rows, sems = rest[-4:]
     rank = interp_ref.shape[-1]
-    part = blocks[0].shape[0] // rank
+    some = blocks[0].shape[0] // rank
     place = lax.axis_index("src")
     scale_rows(warp_ref, rows)
     gains = interp_ref[...].astype(jnp.float32)
@@ -223,14 +232,14 @@
     gains, turns = jnp.concatenate([gains, gains], axis=1), jnp.concatenate([turns, turns], axis=1)
     left = lax.broadcasted_iota(jnp.int32, (1, 2 * rank), 1) < rank
     copies = []
-    for n, k in enumerate(ks):
+    for n, (k, first) in enumerate(items):
         group = place ^ k
 
         def scale_of(m):
-            return rows[pl.ds(group * part + m, 1), :]
-
-        for m in range(0, part, 2):
-            if m + 1 < part:
+            return rows[pl.ds(group * part + first + m, 1), :]
+
+        for m in range(0, some, 2):
+            if m + 1 < some:
                 both = tile(gains, turns, jnp.where(left, scale_of(m), scale_of(m + 1)))
                 none = jnp.zeros_like(both)
                 tiles = jnp.concatenate([jnp.where(left, both, none), jnp.where(left, none, both)], axis=0)
@@ -239,7 +248,7 @@
             else:
                 tiles = tile(gains[:, :rank], turns[:, :rank], scale_of(m)[:, :rank])
                 values[n, m] = product(tiles, blocks[n][m * rank:(m + 1) * rank])
-        copy = pltpu.make_async_copy(values.at[n], out_hbm.at[group], sems.at[n])
+        copy = pltpu.make_async_copy(values.at[n], out_hbm.at[group, first:first + some], sems.at[n])
         copy.start()
         copies.append(copy)
     for copy in copies:
@@ -253,11 +262,12 @@
     group_bits = groups.bit_length() - 1
     part = total // groups
     halves = min(HALVES, part)
+    some = part // halves
     bf16, f32 = jnp.bfloat16, jnp.float32
     params = pltpu.CompilerParams(vmem_limit_bytes=VMEM_LIMIT)
     warp = warp.reshape(1, total)
-    block = jax.ShapeDtypeStruct((part * rank, width), bf16)
-    long_block = jax.ShapeDtypeStruct((part * rank + WARP_ROWS, width), bf16)
+    block = jax.ShapeDtypeStruct((some * rank, width), bf16)
+    long_block = jax.ShapeDtypeStruct((some * rank + WARP_ROWS, width), bf16)
     both_tables = [pltpu.VMEM((2, 2 * rank, 2 * rank), f32)] * 2
     far, near = list(range(groups // 2, groups)), list(range(1, groups // 2))
     order = [k for pair in zip(far, near) for k in pair] + far[len(near):]
@@ -272,10 +282,10 @@
         return lax.ppermute(value, "src", [(i, i ^ k) for i in range(groups)])
 
     blocks = pl.pallas_call(
-        functools.partial(local_kernel, groups, min(GROUP_BITS, bits)),
-        out_shape=[long_block] * groups,
+        functools.partial(local_kernel, groups, halves, min(GROUP_BITS, bits)),
+        out_shape=[long_block] * groups + [block] * ((halves - 1) * groups),
         in_specs=[HBM] * 4,
-        out_specs=[VMEM] * groups,
+        out_specs=[VMEM] * (halves * groups),
         scratch_shapes=[
             pltpu.VMEM(warp.shape, warp.dtype),
             pltpu.VMEM(interp.shape, interp.dtype),
@@ -287,64 +297,64 @@
             pltpu.VMEM((bits, total // 2, 2 * rank, 2 * rank), bf16),
             pltpu.SemaphoreType.DMA((4,)),
         ],
-        compiler_params=params,
+        compiler_params=pltpu.CompilerParams(vmem_limit_bytes=LOCAL_VMEM_LIMIT),
         cost_estimate=cost(total // 2 * bits),
         name="local",
     )(warp, interp, omega, sources)
-    arrived = {0: blocks[0]}
-    for k in order:
-        arrived[k] = moved(blocks[k], k)
-    known = [0] + order[:-1]
-    all_warp = jnp.concatenate([arrived[k][part * rank:part * rank + 1, :total] for k in known], axis=0)
+    def exchanged(blocks):
+        arrived = {0: blocks[0]}
+        for k in order:
+            arrived[k] = moved(blocks[k], k)
+        return arrived
+
+    arrived = [exchanged(blocks[half * groups:(half + 1) * groups]) for half in range(halves)]
+    known = [0] + order[:KNOWN] if groups > KNOWN + 1 else list(range(groups - 1))
+    all_warp = jnp.concatenate([arrived[0][k][some * rank:some * rank + 1, :total] for k in known], axis=0)
     tiles, last_tiles = pl.pallas_call(
         functools.partial(tiles_kernel, part, bits, known),
         out_shape=[
-            jax.ShapeDtypeStruct((group_bits, total - part, rank, 2 * rank), bf16),
-            jax.ShapeDtypeStruct((total - part, rank, 2 * rank), bf16),
+            jax.ShapeDtypeStruct((group_bits, len(known) * part, rank, 2 * rank), bf16),
+            jax.ShapeDtypeStruct((len(known) * part, rank, 2 * rank), bf16),
         ],
         in_specs=[VMEM, VMEM, VMEM],
         out_specs=[VMEM, VMEM],
-        scratch_shapes=both_tables + [pltpu.VMEM((part, groups - 1, LANES), f32)],
+        scratch_shapes=both_tables + [pltpu.VMEM((part, len(known), LANES), f32)],
         compiler_params=params,
         cost_estimate=cost(total // 2 * (group_bits + 1)),
         name="remote_tiles",
     )(all_warp, interp, omega)
-    last_rows = pltpu.VMEM((part, WARP_ROWS, LANES), f32)
-    last_block = arrived[groups - 1]
-    states = []
+    late_rows = pltpu.VMEM((groups - len(known), part, WARP_ROWS, LANES), f32)
+    late = [arrived[0][k] for k in range(groups) if k not in known]
+    returned = []
     for half in range(halves):
-        first_m = half * (part // halves)
-        by_k = [arrived[k] for k in range(groups)]
-        if half:
-            by_k[0] = after(by_k[0], states[0])
-        states.append(pl.pallas_call(
-            functools.partial(remote_kernel, groups, first_m, bits),
-            out_shape=jax.ShapeDtypeStruct((total // halves, rank, width), bf16),
-            in_specs=[VMEM] * (3 + groups),
+        state = pl.pallas_call(
+            functools.partial(remote_kernel, groups, half * some, part, bits, known),
+            out_shape=jax.ShapeDtypeStruct((groups * some, rank, width), bf16),
+            in_specs=[VMEM] * (3 + groups + len(late)),
             out_specs=VMEM,
-            scratch_shapes=both_tables + [last_rows],
+            scratch_shapes=both_tables + [late_rows],
             compiler_params=params,
             cost_estimate=cost(total // 2 // halves * group_bits),
             name=f"remote_{half}",
-        )(tiles, interp, omega, *by_k))
-    others = [lax.ppermute(state, "tgt", [(i, i ^ 1) for i in range(lax.axis_size("tgt"))]) for state in states]
-    blocks = pl.pallas_call(
-        functools.partial(core_kernel, groups, halves, bits + group_bits),
-        out_shape=[block] * groups,
-        in_specs=[VMEM] * (4 + 2 * halves),
-        out_specs=[VMEM] * groups,
-        scratch_shapes=both_tables + [last_rows],
-        compiler_params=params,
-        cost_estimate=cost(total // 2),
-        name="core",
-    )(last_tiles, last_block, interp, omega, *states, *others)
-    arrived = {0: blocks[0]}
-    for k in order:
-        arrived[k] = moved(blocks[k], k)
-    early = [0] + order[:len(order) // 2]
+        )(tiles, interp, omega, *[arrived[half][k] for k in range(groups)], *late)
+        other = lax.ppermute(state, "tgt", [(i, i ^ 1) for i in range(lax.axis_size("tgt"))])
+        blocks = pl.pallas_call(
+            functools.partial(core_kernel, groups, half * some, part, bits + group_bits, known),
+            out_shape=[block] * groups,
+            in_specs=[VMEM] * (5 + len(late)),
+            out_specs=[VMEM] * groups,
+            scratch_shapes=both_tables + [late_rows],
+            compiler_params=params,
+            cost_estimate=cost(total // 2 // halves),
+            name=f"core_{half}",
+        )(last_tiles, interp, omega, state, other, *late)
+        returned.append(exchanged(blocks))
     values = None
-    for name, ks in (("early", early), ("late", [k for k in order if k not in early])):
-        operands = [warp, eval_interp, eval_omega] + [arrived[k] for k in ks]
+    items = [(k, half) for half in range(halves) for k in [0] + order]
+    cuts = [0, len(items) // 2, len(items) - len(order) // 2, len(items)]
+    for i, (start, stop) in enumerate(zip(cuts, cuts[1:])):
+        chosen = items[start:stop]
+        operands = [warp, eval_interp, eval_omega] + [returned[half][k] for k, half in chosen]
         specs = [VMEM] * len(operands)
         aliases = {}
         if values is not None:
@@ -352,19 +362,19 @@
             operands.append(values)
             specs.append(ANY)
         values = pl.pallas_call(
-            functools.partial(eval_kernel, ks),
+            functools.partial(eval_kernel, part, [(k, half * some) for k, half in chosen]),
             out_shape=jax.ShapeDtypeStruct((groups, part, rank, width), f32),
             in_specs=specs,
             out_specs=ANY,
             scratch_shapes=[
-                pltpu.VMEM((len(ks), part, rank, width), f32),
+                pltpu.VMEM((len(chosen), some, rank, width), f32),
                 pltpu.VMEM((total, LANES), f32),
-                pltpu.SemaphoreType.DMA((len(ks),)),
+                pltpu.SemaphoreType.DMA((len(chosen),)),
             ],
             input_output_aliases=aliases,
             compiler_params=params,
-            cost_estimate=cost(len(ks) * part // 2),
-            name=f"eval_{name}",
+            cost_estimate=cost(len(chosen)),
+            name=f"eval_{i}",
         )(*operands)
     return values.reshape(total, rank, width)
 

time: 120 us -> 117 us (0.975)
  the two profiles are of different devices: /device:TPU:16 before, /device:TPU:0 now
where the time goes in v1:
time: 117 us
  starting transfers between devices  56.8 us (49%)
  waiting for transfers between devices  36.3 us (31%)
  Pallas kernels  19.9 us (17%)
  local copies, waits for them, and re-layouts  3.39 us (3%)
    ppermute x28, starting transfers between devices, moved(): return lax.ppermute(value, 'src', [(i, i ^ k) for i in range(groups)])  56.7 us
    ppermute x28, waiting for transfers between devices, moved(): return lax.ppermute(value, 'src', [(i, i ^ k) for i in range(groups)])  36.3 us
    pallas_call x1, Pallas kernels, on_device(): pl.pallas_call(functools.partial(local_kernel, groups, halves, min(GROUP_...  8.76 us
    pallas_call x3, Pallas kernels, on_device(): pl.pallas_call(functools.partial(eval_kernel, part, [(k, half * some) for...  4.28 us
    pallas_call x1, Pallas kernels, on_device(): pl.pallas_call(functools.partial(tiles_kernel, part, bits, known), out_sh...  3.05 us
    unnamed x14, local copies, waits for them, and re-layouts  2.67 us
    pallas_call x2, Pallas kernels, on_device(): pl.pallas_call(functools.partial(remote_kernel, groups, half * some, part...  2.55 us
  transfers between devices with their start and end apart: 30, of which 10 were waited for; matrix products, arithmetic and copies ran while one was open for 1% of the time, Pallas kernels for 8%

profile of v1, /device:TPU:0, one launch (start us, length us, event | category | flops | bytes accessed | tf_op | source)
XLA Modules:
  0.0 116.7 jit_solution(17122166947027217101)
XLA Ops:
  0.0 8.8 %local.1 = (bf16[272,256]{1,0:T(8,128)(2,1)}, bf16[272,256]{1,0:T(8,128)(2,1)}, bf16[272,256]{1,0:T(8,128)(2,1)}, bf16[272,256]{1,0:T(8,128)(2,1)}, bf16[272,256...) custom-call(bf16[1,64]{1,0:T(2,128)(2,1)} %bitcast.2, ...), custom_call_target="tpu_custom_call" | custom-call | flops 192 | bytes 192 | tf_op jit(solution)/shard_map/local/pallas_call | solution.py:284
  8.8 4.1 %collective-permute-start = (bf16[272,256]{1,0:T(8,128)(2,1)}, bf16[272,256]{1,0:T(8,128)(2,1)S(1)}, u32[]{:S(2)}, u32[]{:S(2)}) collective-permute-start(bf16[272,256]{1,0:T(8,128)(2,1)} %get-tuple-element.40), channel_id=1, source_target_pairs={{0,8},{2,10},{4,12},{6,14},{8,0},{10,2},{12,4},{14,6},{1,9},{3,11}... | collective-permute-start | bytes 417800 | tf_op jit(solution)/shard_map/ppermute | solution.py:282
  12.9 1.5 %collective-permute-start.1 = (bf16[272,256]{1,0:T(8,128)(2,1)}, bf16[272,256]{1,0:T(8,128)(2,1)S(1)}, u32[]{:S(2)}, u32[]{:S(2)}) collective-permute-start(bf16[272,256]{1,0:T(8,128)(2,1)} %get-tuple-element.41), channel_id=1, source_target_pairs={{0,2},{2,0},{4,6},{6,4},{8,10},{10,8},{12,14},{14,12},{1,3},{3,1},... | collective-permute-start | bytes 417800 | tf_op jit(solution)/shard_map/ppermute | solution.py:282
  14.4 1.8 %collective-permute-start.4 = (bf16[256,256]{1,0:T(8,128)(2,1)}, bf16[256,256]{1,0:T(8,128)(2,1)S(1)}, u32[]{:S(2)}, u32[]{:S(2)}) collective-permute-start(bf16[256,256]{1,0:T(8,128)(2,1)} %get-tuple-element.47), channel_id=1, source_target_pairs={{0,2},{2,0},{4,6},{6,4},{8,10},{10,8},{12,14},{14,12},{1,3},{3,1},... | collective-permute-start | bytes 393224 | tf_op jit(solution)/shard_map/ppermute | solution.py:282
  16.2 1.6 %collective-permute-start.3 = (bf16[272,256]{1,0:T(8,128)(2,1)}, bf16[272,256]{1,0:T(8,128)(2,1)S(1)}, u32[]{:S(2)}, u32[]{:S(2)}) collective-permute-start(bf16[272,256]{1,0:T(8,128)(2,1)} %get-tuple-element.43), channel_id=1, source_target_pairs={{0,4},{2,6},{4,0},{6,2},{8,12},{10,14},{12,8},{14,10},{1,5},{3,7},... | collective-permute-start | bytes 417800 | tf_op jit(solution)/shard_map/ppermute | solution.py:282
  17.8 3.3 %collective-permute-done.4.rest_1_ = bf16[256,256]{1,0:T(8,128)(2,1)S(1)} collective-permute-done((bf16[256,256]{1,0:T(8,128)(2,1)}, bf16[256,256]{1,0:T(8,128)(2,1)S(1)}, u32[]{:S(2)}, u32[]{:S(2)}) %collective-permute-start.4) | collective-permute-done | bytes 131104 | tf_op jit(solution)/shard_map/ppermute | solution.py:282
  21.0 5.5 %collective-permute-start.11 = (bf16[272,256]{1,0:T(8,128)(2,1)}, bf16[272,256]{1,0:T(8,128)(2,1)S(1)}, u32[]{:S(2)}, u32[]{:S(2)}) collective-permute-start(bf16[272,256]{1,0:T(8,128)(2,1)} %get-tuple-element.54), channel_id=1, source_target_pairs={{0,6},{2,4},{4,2},{6,0},{8,14},{10,12},{12,10},{14,8},{1,7},{3,5},... | collective-permute-start | bytes 417800 | tf_op jit(solution)/shard_map/ppermute | solution.py:282
  26.9 3.4 %collective-permute-start.13 = (bf16[272,256]{1,0:T(8,128)(2,1)}, bf16[272,256]{1,0:T(8,128)(2,1)S(1)}, u32[]{:S(2)}, u32[]{:S(2)}) collective-permute-start(bf16[272,256]{1,0:T(8,128)(2,1)} %get-tuple-element.56), channel_id=1, source_target_pairs={{0,14},{2,12},{4,10},{6,8},{8,6},{10,4},{12,2},{14,0},{1,15},{3,13... | collective-permute-start | bytes 417800 | tf_op jit(solution)/shard_map/ppermute | solution.py:282
  30.3 3.0 %collective-permute-start.6 = (bf16[256,256]{1,0:T(8,128)(2,1)}, bf16[256,256]{1,0:T(8,128)(2,1)S(1)}, u32[]{:S(2)}, u32[]{:S(2)}) collective-permute-start(bf16[256,256]{1,0:T(8,128)(2,1)} %get-tuple-element.49), channel_id=1, source_target_pairs={{0,6},{2,4},{4,2},{6,0},{8,14},{10,12},{12,10},{14,8},{1,7},{3,5},... | collective-permute-start | bytes 393224 | tf_op jit(solution)/shard_map/ppermute | solution.py:282
  35.8 3.1 %remote_tiles.1 = (bf16[3,40,64,128]{3,2,1,0:T(8,128)(2,1)S(1)}, bf16[40,64,128]{2,1,0:T(8,128)(2,1)S(1)}) custom-call(bf16[5,64]{1,0:T(8,128)(2,1)S(1)} %concatenate.3.warp_ref, bf16[2,2,64,64]{3,2,1,0:T(8,128)(2,1)S(1)} %copy-done.1, f32[2,2,64,64]{3,2,1,0:T(8,128)S(1)} %copy-done), custom_call_target="tpu_custom_call" | custom-call | flops 128 | bytes 128 | tf_op jit(solution)/shard_map/remote_tiles/pallas_call | solution.py:313
  39.2 1.9 %collective-permute-start.7 = (bf16[256,256]{1,0:T(8,128)(2,1)}, bf16[256,256]{1,0:T(8,128)(2,1)S(1)}, u32[]{:S(2)}, u32[]{:S(2)}) collective-permute-start(bf16[256,256]{1,0:T(8,128)(2,1)} %get-tuple-element.50), channel_id=1, source_target_pairs={{0,8},{2,10},{4,12},{6,14},{8,0},{10,2},{12,4},{14,6},{1,9},{3,11}... | collective-permute-start | bytes 393224 | tf_op jit(solution)/shard_map/ppermute | solution.py:282
  42.3 3.5 %collective-permute-start.9 = (bf16[256,256]{1,0:T(8,128)(2,1)}, bf16[256,256]{1,0:T(8,128)(2,1)S(1)}, u32[]{:S(2)}, u32[]{:S(2)}) collective-permute-start(bf16[256,256]{1,0:T(8,128)(2,1)} %get-tuple-element.52), channel_id=1, source_target_pairs={{0,12},{2,14},{4,8},{6,10},{8,4},{10,6},{12,0},{14,2},{1,13},{3,15... | collective-permute-start | bytes 393224 | tf_op jit(solution)/shard_map/ppermute | solution.py:282
  49.0 7.5 %collective-permute-done.7.rest_4_ = bf16[256,256]{1,0:T(8,128)(2,1)S(1)} collective-permute-done((bf16[256,256]{1,0:T(8,128)(2,1)}, bf16[256,256]{1,0:T(8,128)(2,1)S(1)}, u32[]{:S(2)}, u32[]{:S(2)}) %collective-permute-start.7) | collective-permute-done | bytes 131104 | tf_op jit(solution)/shard_map/ppermute | solution.py:282
  56.5 3.8 %collective-permute-done.8.rest_5_ = bf16[256,256]{1,0:T(8,128)(2,1)S(1)} collective-permute-done((bf16[256,256]{1,0:T(8,128)(2,1)}, bf16[256,256]{1,0:T(8,128)(2,1)S(1)}, u32[]{:S(2)}, u32[]{:S(2)}) %collective-permute-start.8) | collective-permute-done | bytes 131104 | tf_op jit(solution)/shard_map/ppermute | solution.py:282
  60.3 1.4 %remote_1.1.own = bf16[32,64,256]{2,1,0:T(8,128)(2,1)S(1)} custom-call(bf16[3,40,64,128]{3,2,1,0:T(8,128)(2,1)S(1)} %get-tuple-element.45.tiles, bf16[2,2,64,64]{3,2,1,0:T(8,128)(2,1)S(1)} %copy-done.1, f32[2,2,64,64]{3,2,1,0:T(8,128)S(1)} %copy-done, bf16[256,256]{1,0:T(8,128)(2,1)S(1)} %copy-done.5, bf16[256,256]{1,0:T(8,128)(2,1)S(1)} %collective-permute-done.4.rest_1_, ...), custom_call_target="tpu_custom_call" | custom-call | flops 48 | bytes 48 | tf_op jit(solution)/shard_map/remote_1/pallas_call | solution.py:330
  62.4 6.4 %collective-permute-start.23 = (bf16[256,256]{1,0:T(8,128)(2,1)S(1)}, bf16[256,256]{1,0:T(8,128)(2,1)S(1)}, u32[]{:S(2)}, u32[]{:S(2)}) collective-permute-start(bf16[256,256]{1,0:T(8,128)(2,1)S(1)} %get-tuple-element.66), channel_id=1, source_target_pairs={{0,8},{2,10},{4,12},{6,14},{8,0},{10,2},{12,4},{14,6},{1,9},{3,11}... | collective-permute-start | bytes 393224 | tf_op jit(solution)/shard_map/ppermute | solution.py:282
  70.3 2.1 %collective-permute-start.26 = (bf16[256,256]{1,0:T(8,128)(2,1)S(1)}, bf16[256,256]{1,0:T(8,128)(2,1)S(1)}, u32[]{:S(2)}, u32[]{:S(2)}) collective-permute-start(bf16[256,256]{1,0:T(8,128)(2,1)S(1)} %get-tuple-element.69), channel_id=1, source_target_pairs={{0,4},{2,6},{4,0},{6,2},{8,12},{10,14},{12,8},{14,10},{1,5},{3,7},... | collective-permute-start | bytes 393224 | tf_op jit(solution)/shard_map/ppermute | solution.py:282
  72.4 2.2 %collective-permute-start.27 = (bf16[256,256]{1,0:T(8,128)(2,1)S(1)}, bf16[256,256]{1,0:T(8,128)(2,1)S(1)}, u32[]{:S(2)}, u32[]{:S(2)}) collective-permute-start(bf16[256,256]{1,0:T(8,128)(2,1)S(1)} %get-tuple-element.70), channel_id=1, source_target_pairs={{0,12},{2,14},{4,8},{6,10},{8,4},{10,6},{12,0},{14,2},{1,13},{3,15... | collective-permute-start | bytes 393224 | tf_op jit(solution)/shard_map/ppermute | solution.py:282
  75.3 3.5 %collective-permute-done.23.rest_1_ = bf16[256,256]{1,0:T(8,128)(2,1)S(1)} collective-permute-done((bf16[256,256]{1,0:T(8,128)(2,1)S(1)}, bf16[256,256]{1,0:T(8,128)(2,1)S(1)}, u32[]{:S(2)}, u32[]{:S(2)}) %collective-permute-start.23) | collective-permute-done | bytes 131104 | tf_op jit(solution)/shard_map/ppermute | solution.py:282
  78.8 2.0 %collective-permute-start.29 = (bf16[256,256]{1,0:T(8,128)(2,1)S(1)}, bf16[256,256]{1,0:T(8,128)(2,1)S(1)}, u32[]{:S(2)}, u32[]{:S(2)}) collective-permute-start(bf16[256,256]{1,0:T(8,128)(2,1)S(1)} %get-tuple-element.72), channel_id=1, source_target_pairs={{0,14},{2,12},{4,10},{6,8},{8,6},{10,4},{12,2},{14,0},{1,15},{3,13... | collective-permute-start | bytes 393224 | tf_op jit(solution)/shard_map/ppermute | solution.py:282
  80.8 3.9 %collective-permute-done.25.rest_3_ = bf16[256,256]{1,0:T(8,128)(2,1)S(1)} collective-permute-done((bf16[256,256]{1,0:T(8,128)(2,1)S(1)}, bf16[256,256]{1,0:T(8,128)(2,1)S(1)}, u32[]{:S(2)}, u32[]{:S(2)}) %collective-permute-start.25) | collective-permute-done | bytes 131104 | tf_op jit(solution)/shard_map/ppermute | solution.py:282
  84.6 1.3 %collective-permute-start.19 = (bf16[256,256]{1,0:T(8,128)(2,1)S(1)}, bf16[256,256]{1,0:T(8,128)(2,1)S(1)}, u32[]{:S(2)}, u32[]{:S(2)}) collective-permute-start(bf16[256,256]{1,0:T(8,128)(2,1)S(1)} %get-tuple-element.62), channel_id=1, source_target_pairs={{0,2},{2,0},{4,6},{6,4},{8,10},{10,8},{12,14},{14,12},{1,3},{3,1},... | collective-permute-start | bytes 393224 | tf_op jit(solution)/shard_map/ppermute | solution.py:282
  85.9 1.6 %collective-permute-start.15 = (bf16[256,256]{1,0:T(8,128)(2,1)S(1)}, bf16[256,256]{1,0:T(8,128)(2,1)S(1)}, u32[]{:S(2)}, u32[]{:S(2)}) collective-permute-start(bf16[256,256]{1,0:T(8,128)(2,1)S(1)} %get-tuple-element.57), channel_id=1, source_target_pairs={{0,12},{2,14},{4,8},{6,10},{8,4},{10,6},{12,0},{14,2},{1,13},{3,15... | collective-permute-start | bytes 393224 | tf_op jit(solution)/shard_map/ppermute | solution.py:282
  87.5 2.6 %collective-permute-done.28.rest_6_ = bf16[256,256]{1,0:T(8,128)(2,1)S(1)} collective-permute-done((bf16[256,256]{1,0:T(8,128)(2,1)S(1)}, bf16[256,256]{1,0:T(8,128)(2,1)S(1)}, u32[]{:S(2)}, u32[]{:S(2)}) %collective-permute-start.28) | collective-permute-done | bytes 131104 | tf_op jit(solution)/shard_map/ppermute | solution.py:282
  90.1 7.8 %collective-permute-start.20 = (bf16[256,256]{1,0:T(8,128)(2,1)S(1)}, bf16[256,256]{1,0:T(8,128)(2,1)S(1)}, u32[]{:S(2)}, u32[]{:S(2)}) collective-permute-start(bf16[256,256]{1,0:T(8,128)(2,1)S(1)} %get-tuple-element.63), channel_id=1, source_target_pairs={{0,10},{2,8},{4,14},{6,12},{8,2},{10,0},{12,6},{14,4},{1,11},{3,9}... | collective-permute-start | bytes 393224 | tf_op jit(solution)/shard_map/ppermute | solution.py:282
  97.9 1.3 %collective-permute-start.21 = (bf16[256,256]{1,0:T(8,128)(2,1)S(1)}, bf16[256,256]{1,0:T(8,128)(2,1)S(1)}, u32[]{:S(2)}, u32[]{:S(2)}) collective-permute-start(bf16[256,256]{1,0:T(8,128)(2,1)S(1)} %get-tuple-element.64), channel_id=1, source_target_pairs={{0,4},{2,6},{4,0},{6,2},{8,12},{10,14},{12,8},{14,10},{1,5},{3,7},... | collective-permute-start | bytes 393224 | tf_op jit(solution)/shard_map/ppermute | solution.py:282
  99.2 4.8 %collective-permute-done.18.rest_1_ = bf16[256,256]{1,0:T(8,128)(2,1)S(1)} collective-permute-done((bf16[256,256]{1,0:T(8,128)(2,1)S(1)}, bf16[256,256]{1,0:T(8,128)(2,1)S(1)}, u32[]{:S(2)}, u32[]{:S(2)}) %collective-permute-start.18) | collective-permute-done | bytes 131104 | tf_op jit(solution)/shard_map/ppermute | solution.py:282
  104.1 1.5 %collective-permute-start.17 = (bf16[256,256]{1,0:T(8,128)(2,1)S(1)}, bf16[256,256]{1,0:T(8,128)(2,1)S(1)}, u32[]{:S(2)}, u32[]{:S(2)}) collective-permute-start(bf16[256,256]{1,0:T(8,128)(2,1)S(1)} %get-tuple-element.59), channel_id=1, source_target_pairs={{0,14},{2,12},{4,10},{6,8},{8,6},{10,4},{12,2},{14,0},{1,15},{3,13... | collective-permute-start | bytes 393224 | tf_op jit(solution)/shard_map/ppermute | solution.py:282
  105.6 1.7 %eval_0.1.rest_5_ = f32[8,8,64,256]{3,2,1,0:T(8,128)} custom-call(bf16[1,64]{1,0:T(2,128)(2,1)S(1)} %bitcast.3, bf16[64,64]{1,0:T(8,128)(2,1)S(1)} %copy-done.3, f32[64,64]{1,0:T(8,128)S(1)} %copy-done.2, bf16[256,256]{1,0:T(8,128)(2,1)S(1)} %get-tuple-element.65.rest_0_, bf16[256,256]{1,0:T(8,128)(2,1)S(1)} %collective-permute-done.23.rest_1_, ...), custom_call_target="tpu_custom_call" | custom-call | flops 8 | bytes 8 | tf_op jit(solution)/shard_map/eval_0/pallas_call | solution.py:364
  107.3 5.4 %collective-permute-done.20.rest_3_ = bf16[256,256]{1,0:T(8,128)(2,1)S(1)} collective-permute-done((bf16[256,256]{1,0:T(8,128)(2,1)S(1)}, bf16[256,256]{1,0:T(8,128)(2,1)S(1)}, u32[]{:S(2)}, u32[]{:S(2)}) %collective-permute-start.20) | collective-permute-done | bytes 131104 | tf_op jit(solution)/shard_map/ppermute | solution.py:282
  112.8 1.4 %eval_1.1.rest_3_ = f32[8,8,64,256]{3,2,1,0:T(8,128)} custom-call(bf16[1,64]{1,0:T(2,128)(2,1)S(1)} %bitcast.4, bf16[64,64]{1,0:T(8,128)(2,1)S(1)} %copy-done.3, f32[64,64]{1,0:T(8,128)S(1)} %copy-done.2, bf16[256,256]{1,0:T(8,128)(2,1)S(1)} %get-tuple-element.60.rest_0_, ...), custom_call_target="tpu_custom_call", output_to_operand_aliasing={{}: (8, {})} | custom-call | flops 5 | bytes 5 | tf_op jit(solution)/shard_map/eval_1/pallas_call | solution.py:364
  115.3 1.2 %eval_2.1 = f32[8,8,64,256]{3,2,1,0:T(8,128)} custom-call(bf16[1,64]{1,0:T(2,128)(2,1)S(1)} %bitcast.5, bf16[64,64]{1,0:T(8,128)(2,1)S(1)} %copy-done.3, f32[64,64]{1,0:T(8,128)S(1)} %copy-done.2, bf16[256,256]{1,0:T(8,128)(2,1)S(1)} %collective-permute-done.15.rest_0_, ...), custom_call_target="tpu_custom_call", output_to_operand_aliasing={{}: (6, {})} | custom-call | flops 3 | bytes 3 | tf_op jit(solution)/shard_map/eval_2/pallas_call | solution.py:364
  (57 shorter events, 11.6 us)
Async XLA Ops:
  8.8 17.8 %collective-permute-start = (bf16[272,256]{1,0:T(8,128)(2,1)}, bf16[272,256]{1,0:T(8,128)(2,1)S(1)}, u32[]{:S(2)}, u32[]{:S(2)}) collective-permute-start(bf16[272,256]{1,0:T(8,128)(2,1)} %get-tuple-element.40), channel_id=1, source_target_pairs={{0,8},{2,10},{4,12},{6,14},{8,0},{10,2},{12,4},{14,6},{1,9},{3,11}... | collective-permute-start | bytes 417800 | tf_op jit(solution)/shard_map/ppermute | solution.py:282
  12.9 14.0 %collective-permute-start.1 = (bf16[272,256]{1,0:T(8,128)(2,1)}, bf16[272,256]{1,0:T(8,128)(2,1)S(1)}, u32[]{:S(2)}, u32[]{:S(2)}) collective-permute-start(bf16[272,256]{1,0:T(8,128)(2,1)} %get-tuple-element.41), channel_id=1, source_target_pairs={{0,2},{2,0},{4,6},{6,4},{8,10},{10,8},{12,14},{14,12},{1,3},{3,1},... | collective-permute-start | bytes 417800 | tf_op jit(solution)/shard_map/ppermute | solution.py:282
  14.4 15.9 %collective-permute-start.2 = (bf16[272,256]{1,0:T(8,128)(2,1)}, bf16[272,256]{1,0:T(8,128)(2,1)S(1)}, u32[]{:S(2)}, u32[]{:S(2)}) collective-permute-start(bf16[272,256]{1,0:T(8,128)(2,1)} %get-tuple-element.42), channel_id=1, source_target_pairs={{0,10},{2,8},{4,14},{6,12},{8,2},{10,0},{12,6},{14,4},{1,11},{3,9}... | collective-permute-start | bytes 417800 | tf_op jit(solution)/shard_map/ppermute | solution.py:282
  14.4 6.6 %collective-permute-start.4 = (bf16[256,256]{1,0:T(8,128)(2,1)}, bf16[256,256]{1,0:T(8,128)(2,1)S(1)}, u32[]{:S(2)}, u32[]{:S(2)}) collective-permute-start(bf16[256,256]{1,0:T(8,128)(2,1)} %get-tuple-element.47), channel_id=1, source_target_pairs={{0,2},{2,0},{4,6},{6,4},{8,10},{10,8},{12,14},{14,12},{1,3},{3,1},... | collective-permute-start | bytes 393224 | tf_op jit(solution)/shard_map/ppermute | solution.py:282
  16.2 14.1 %collective-permute-start.3 = (bf16[272,256]{1,0:T(8,128)(2,1)}, bf16[272,256]{1,0:T(8,128)(2,1)S(1)}, u32[]{:S(2)}, u32[]{:S(2)}) collective-permute-start(bf16[272,256]{1,0:T(8,128)(2,1)} %get-tuple-element.43), channel_id=1, source_target_pairs={{0,4},{2,6},{4,0},{6,2},{8,12},{10,14},{12,8},{14,10},{1,5},{3,7},... | collective-permute-start | bytes 417800 | tf_op jit(solution)/shard_map/ppermute | solution.py:282
  21.0 20.1 %collective-permute-start.11 = (bf16[272,256]{1,0:T(8,128)(2,1)}, bf16[272,256]{1,0:T(8,128)(2,1)S(1)}, u32[]{:S(2)}, u32[]{:S(2)}) collective-permute-start(bf16[272,256]{1,0:T(8,128)(2,1)} %get-tuple-element.54), channel_id=1, source_target_pairs={{0,6},{2,4},{4,2},{6,0},{8,14},{10,12},{12,10},{14,8},{1,7},{3,5},... | collective-permute-start | bytes 417800 | tf_op jit(solution)/shard_map/ppermute | solution.py:282
  26.5 15.8 %collective-permute-start.12 = (bf16[272,256]{1,0:T(8,128)(2,1)}, bf16[272,256]{1,0:T(8,128)(2,1)S(1)}, u32[]{:S(2)}, u32[]{:S(2)}) collective-permute-start(bf16[272,256]{1,0:T(8,128)(2,1)} %get-tuple-element.55), channel_id=1, source_target_pairs={{0,12},{2,14},{4,8},{6,10},{8,4},{10,6},{12,0},{14,2},{1,13},{3,15... | collective-permute-start | bytes 417800 | tf_op jit(solution)/shard_map/ppermute | solution.py:282
  26.9 18.9 %collective-permute-start.13 = (bf16[272,256]{1,0:T(8,128)(2,1)}, bf16[272,256]{1,0:T(8,128)(2,1)S(1)}, u32[]{:S(2)}, u32[]{:S(2)}) collective-permute-start(bf16[272,256]{1,0:T(8,128)(2,1)} %get-tuple-element.56), channel_id=1, source_target_pairs={{0,14},{2,12},{4,10},{6,8},{8,6},{10,4},{12,2},{14,0},{1,15},{3,13... | collective-permute-start | bytes 417800 | tf_op jit(solution)/shard_map/ppermute | solution.py:282
  30.3 8.9 %collective-permute-start.5 = (bf16[256,256]{1,0:T(8,128)(2,1)}, bf16[256,256]{1,0:T(8,128)(2,1)S(1)}, u32[]{:S(2)}, u32[]{:S(2)}) collective-permute-start(bf16[256,256]{1,0:T(8,128)(2,1)} %get-tuple-element.48), channel_id=1, source_target_pairs={{0,4},{2,6},{4,0},{6,2},{8,12},{10,14},{12,8},{14,10},{1,5},{3,7},... | collective-permute-start | bytes 393224 | tf_op jit(solution)/shard_map/ppermute | solution.py:282
  30.3 18.6 %collective-permute-start.6 = (bf16[256,256]{1,0:T(8,128)(2,1)}, bf16[256,256]{1,0:T(8,128)(2,1)S(1)}, u32[]{:S(2)}, u32[]{:S(2)}) collective-permute-start(bf16[256,256]{1,0:T(8,128)(2,1)} %get-tuple-element.49), channel_id=1, source_target_pairs={{0,6},{2,4},{4,2},{6,0},{8,14},{10,12},{12,10},{14,8},{1,7},{3,5},... | collective-permute-start | bytes 393224 | tf_op jit(solution)/shard_map/ppermute | solution.py:282
  39.2 17.3 %collective-permute-start.7 = (bf16[256,256]{1,0:T(8,128)(2,1)}, bf16[256,256]{1,0:T(8,128)(2,1)S(1)}, u32[]{:S(2)}, u32[]{:S(2)}) collective-permute-start(bf16[256,256]{1,0:T(8,128)(2,1)} %get-tuple-element.50), channel_id=1, source_target_pairs={{0,8},{2,10},{4,12},{6,14},{8,0},{10,2},{12,4},{14,6},{1,9},{3,11}... | collective-permute-start | bytes 393224 | tf_op jit(solution)/shard_map/ppermute | solution.py:282
  41.1 19.2 %collective-permute-start.8 = (bf16[256,256]{1,0:T(8,128)(2,1)}, bf16[256,256]{1,0:T(8,128)(2,1)S(1)}, u32[]{:S(2)}, u32[]{:S(2)}) collective-permute-start(bf16[256,256]{1,0:T(8,128)(2,1)} %get-tuple-element.51), channel_id=1, source_target_pairs={{0,10},{2,8},{4,14},{6,12},{8,2},{10,0},{12,6},{14,4},{1,11},{3,9}... | collective-permute-start | bytes 393224 | tf_op jit(solution)/shard_map/ppermute | solution.py:282
  42.3 18.0 %collective-permute-start.9 = (bf16[256,256]{1,0:T(8,128)(2,1)}, bf16[256,256]{1,0:T(8,128)(2,1)S(1)}, u32[]{:S(2)}, u32[]{:S(2)}) collective-permute-start(bf16[256,256]{1,0:T(8,128)(2,1)} %get-tuple-element.52), channel_id=1, source_target_pairs={{0,12},{2,14},{4,8},{6,10},{8,4},{10,6},{12,0},{14,2},{1,13},{3,15... | collective-permute-start | bytes 393224 | tf_op jit(solution)/shard_map/ppermute | solution.py:282
  45.8 14.5 %collective-permute-start.10 = (bf16[256,256]{1,0:T(8,128)(2,1)}, bf16[256,256]{1,0:T(8,128)(2,1)S(1)}, u32[]{:S(2)}, u32[]{:S(2)}) collective-permute-start(bf16[256,256]{1,0:T(8,128)(2,1)} %get-tuple-element.53), channel_id=1, source_target_pairs={{0,14},{2,12},{4,10},{6,8},{8,6},{10,4},{12,2},{14,0},{1,15},{3,13... | collective-permute-start | bytes 393224 | tf_op jit(solution)/shard_map/ppermute | solution.py:282
  48.9 12.9 %collective-permute-start.22 = (bf16[32,64,256]{2,1,0:T(8,128)(2,1)S(1)}, bf16[32,64,256]{2,1,0:T(8,128)(2,1)S(1)}, u32[]{:S(2)}, u32[]{:S(2)}) collective-permute-start(bf16[32,64,256]{2,1,0:T(8,128)(2,1)S(1)} %remote_0.1.own), channel_id=1, source_target_pairs={{0,1},{1,0},{2,3},{3,2},{4,5},{5,4},{6,7},{7,6},{8,9},{9,8},{10,11... | collective-permute-start | bytes 3145736 | tf_op jit(solution)/shard_map/ppermute | solution.py:340
  61.7 44.0 %copy-start.2 = (f32[64,64]{1,0:T(8,128)S(1)}, f32[64,64]{1,0:T(8,128)}, u32[]{:S(2)}) copy-start(f32[64,64]{1,0:T(8,128)} %omega_ref.15) | copy-start | bytes 49156
  61.7 44.0 %copy-start.3 = (bf16[64,64]{1,0:T(8,128)(2,1)S(1)}, bf16[64,64]{1,0:T(8,128)(2,1)}, u32[]{:S(2)}) copy-start(bf16[64,64]{1,0:T(8,128)(2,1)} %interp_ref.15) | copy-start | bytes 24580
  61.7 10.7 %collective-permute-start.14 = (bf16[32,64,256]{2,1,0:T(8,128)(2,1)S(1)}, bf16[32,64,256]{2,1,0:T(8,128)(2,1)S(1)}, u32[]{:S(2)}, u32[]{:S(2)}) collective-permute-start(bf16[32,64,256]{2,1,0:T(8,128)(2,1)S(1)} %remote_1.1.own), channel_id=1, source_target_pairs={{0,1},{1,0},{2,3},{3,2},{4,5},{5,4},{6,7},{7,6},{8,9},{9,8},{10,11... | collective-permute-start | bytes 3145736 | tf_op jit(solution)/shard_map/ppermute | solution.py:340
  62.4 16.3 %collective-permute-start.23 = (bf16[256,256]{1,0:T(8,128)(2,1)S(1)}, bf16[256,256]{1,0:T(8,128)(2,1)S(1)}, u32[]{:S(2)}, u32[]{:S(2)}) collective-permute-start(bf16[256,256]{1,0:T(8,128)(2,1)S(1)} %get-tuple-element.66), channel_id=1, source_target_pairs={{0,8},{2,10},{4,12},{6,14},{8,0},{10,2},{12,4},{14,6},{1,9},{3,11}... | collective-permute-start | bytes 393224 | tf_op jit(solution)/shard_map/ppermute | solution.py:282
  68.8 10.0 %collective-permute-start.24 = (bf16[256,256]{1,0:T(8,128)(2,1)S(1)}, bf16[256,256]{1,0:T(8,128)(2,1)S(1)}, u32[]{:S(2)}, u32[]{:S(2)}) collective-permute-start(bf16[256,256]{1,0:T(8,128)(2,1)S(1)} %get-tuple-element.67), channel_id=1, source_target_pairs={{0,2},{2,0},{4,6},{6,4},{8,10},{10,8},{12,14},{14,12},{1,3},{3,1},... | collective-permute-start | bytes 393224 | tf_op jit(solution)/shard_map/ppermute | solution.py:282
  69.6 15.1 %collective-permute-start.25 = (bf16[256,256]{1,0:T(8,128)(2,1)S(1)}, bf16[256,256]{1,0:T(8,128)(2,1)S(1)}, u32[]{:S(2)}, u32[]{:S(2)}) collective-permute-start(bf16[256,256]{1,0:T(8,128)(2,1)S(1)} %get-tuple-element.68), channel_id=1, source_target_pairs={{0,10},{2,8},{4,14},{6,12},{8,2},{10,0},{12,6},{14,4},{1,11},{3,9}... | collective-permute-start | bytes 393224 | tf_op jit(solution)/shard_map/ppermute | solution.py:282
  70.3 14.3 %collective-permute-start.26 = (bf16[256,256]{1,0:T(8,128)(2,1)S(1)}, bf16[256,256]{1,0:T(8,128)(2,1)S(1)}, u32[]{:S(2)}, u32[]{:S(2)}) collective-permute-start(bf16[256,256]{1,0:T(8,128)(2,1)S(1)} %get-tuple-element.69), channel_id=1, source_target_pairs={{0,4},{2,6},{4,0},{6,2},{8,12},{10,14},{12,8},{14,10},{1,5},{3,7},... | collective-permute-start | bytes 393224 | tf_op jit(solution)/shard_map/ppermute | solution.py:282
  72.4 13.5 %collective-permute-start.27 = (bf16[256,256]{1,0:T(8,128)(2,1)S(1)}, bf16[256,256]{1,0:T(8,128)(2,1)S(1)}, u32[]{:S(2)}, u32[]{:S(2)}) collective-permute-start(bf16[256,256]{1,0:T(8,128)(2,1)S(1)} %get-tuple-element.70), channel_id=1, source_target_pairs={{0,12},{2,14},{4,8},{6,10},{8,4},{10,6},{12,0},{14,2},{1,13},{3,15... | collective-permute-start | bytes 393224 | tf_op jit(solution)/shard_map/ppermute | solution.py:282
  78.8 11.3 %collective-permute-start.28 = (bf16[256,256]{1,0:T(8,128)(2,1)S(1)}, bf16[256,256]{1,0:T(8,128)(2,1)S(1)}, u32[]{:S(2)}, u32[]{:S(2)}) collective-permute-start(bf16[256,256]{1,0:T(8,128)(2,1)S(1)} %get-tuple-element.71), channel_id=1, source_target_pairs={{0,6},{2,4},{4,2},{6,0},{8,14},{10,12},{12,10},{14,8},{1,7},{3,5},... | collective-permute-start | bytes 393224 | tf_op jit(solution)/shard_map/ppermute | solution.py:282
  78.8 19.1 %collective-permute-start.29 = (bf16[256,256]{1,0:T(8,128)(2,1)S(1)}, bf16[256,256]{1,0:T(8,128)(2,1)S(1)}, u32[]{:S(2)}, u32[]{:S(2)}) collective-permute-start(bf16[256,256]{1,0:T(8,128)(2,1)S(1)} %get-tuple-element.72), channel_id=1, source_target_pairs={{0,14},{2,12},{4,10},{6,8},{8,6},{10,4},{12,2},{14,0},{1,15},{3,13... | collective-permute-start | bytes 393224 | tf_op jit(solution)/shard_map/ppermute | solution.py:282
  84.6 19.5 %collective-permute-start.18 = (bf16[256,256]{1,0:T(8,128)(2,1)S(1)}, bf16[256,256]{1,0:T(8,128)(2,1)S(1)}, u32[]{:S(2)}, u32[]{:S(2)}) collective-permute-start(bf16[256,256]{1,0:T(8,128)(2,1)S(1)} %get-tuple-element.61), channel_id=1, source_target_pairs={{0,8},{2,10},{4,12},{6,14},{8,0},{10,2},{12,4},{14,6},{1,9},{3,11}... | collective-permute-start | bytes 393224 | tf_op jit(solution)/shard_map/ppermute | solution.py:282
  84.6 19.5 %collective-permute-start.19 = (bf16[256,256]{1,0:T(8,128)(2,1)S(1)}, bf16[256,256]{1,0:T(8,128)(2,1)S(1)}, u32[]{:S(2)}, u32[]{:S(2)}) collective-permute-start(bf16[256,256]{1,0:T(8,128)(2,1)S(1)} %get-tuple-element.62), channel_id=1, source_target_pairs={{0,2},{2,0},{4,6},{6,4},{8,10},{10,8},{12,14},{14,12},{1,3},{3,1},... | collective-permute-start | bytes 393224 | tf_op jit(solution)/shard_map/ppermute | solution.py:282
  85.9 28.3 %collective-permute-start.15 = (bf16[256,256]{1,0:T(8,128)(2,1)S(1)}, bf16[256,256]{1,0:T(8,128)(2,1)S(1)}, u32[]{:S(2)}, u32[]{:S(2)}) collective-permute-start(bf16[256,256]{1,0:T(8,128)(2,1)S(1)} %get-tuple-element.57), channel_id=1, source_target_pairs={{0,12},{2,14},{4,8},{6,10},{8,4},{10,6},{12,0},{14,2},{1,13},{3,15... | collective-permute-start | bytes 393224 | tf_op jit(solution)/shard_map/ppermute | solution.py:282
  90.1 22.7 %collective-permute-start.20 = (bf16[256,256]{1,0:T(8,128)(2,1)S(1)}, bf16[256,256]{1,0:T(8,128)(2,1)S(1)}, u32[]{:S(2)}, u32[]{:S(2)}) collective-permute-start(bf16[256,256]{1,0:T(8,128)(2,1)S(1)} %get-tuple-element.63), channel_id=1, source_target_pairs={{0,10},{2,8},{4,14},{6,12},{8,2},{10,0},{12,6},{14,4},{1,11},{3,9}... | collective-permute-start | bytes 393224 | tf_op jit(solution)/shard_map/ppermute | solution.py:282
  97.9 14.9 %collective-permute-start.21 = (bf16[256,256]{1,0:T(8,128)(2,1)S(1)}, bf16[256,256]{1,0:T(8,128)(2,1)S(1)}, u32[]{:S(2)}, u32[]{:S(2)}) collective-permute-start(bf16[256,256]{1,0:T(8,128)(2,1)S(1)} %get-tuple-element.64), channel_id=1, source_target_pairs={{0,4},{2,6},{4,0},{6,2},{8,12},{10,14},{12,8},{14,10},{1,5},{3,7},... | collective-permute-start | bytes 393224 | tf_op jit(solution)/shard_map/ppermute | solution.py:282
  104.1 11.2 %collective-permute-start.16 = (bf16[256,256]{1,0:T(8,128)(2,1)S(1)}, bf16[256,256]{1,0:T(8,128)(2,1)S(1)}, u32[]{:S(2)}, u32[]{:S(2)}) collective-permute-start(bf16[256,256]{1,0:T(8,128)(2,1)S(1)} %get-tuple-element.58), channel_id=1, source_target_pairs={{0,6},{2,4},{4,2},{6,0},{8,14},{10,12},{12,10},{14,8},{1,7},{3,5},... | collective-permute-start | bytes 393224 | tf_op jit(solution)/shard_map/ppermute | solution.py:282
  104.1 11.2 %collective-permute-start.17 = (bf16[256,256]{1,0:T(8,128)(2,1)S(1)}, bf16[256,256]{1,0:T(8,128)(2,1)S(1)}, u32[]{:S(2)}, u32[]{:S(2)}) collective-permute-start(bf16[256,256]{1,0:T(8,128)(2,1)S(1)} %get-tuple-element.59), channel_id=1, source_target_pairs={{0,14},{2,12},{4,10},{6,8},{8,6},{10,4},{12,2},{14,0},{1,15},{3,13... | collective-permute-start | bytes 393224 | tf_op jit(solution)/shard_map/ppermute | solution.py:282
  (5 other events, 71.1 us)

commit v2 on v1

--- a/solution.py
+++ b/solution.py
@@ -270,7 +270,8 @@
     long_block = jax.ShapeDtypeStruct((some * rank + WARP_ROWS, width), bf16)
     both_tables = [pltpu.VMEM((2, 2 * rank, 2 * rank), f32)] * 2
     far, near = list(range(groups // 2, groups)), list(range(1, groups // 2))
-    order = [k for pair in zip(far, near) for k in pair] + far[len(near):]
+    far_order, near_order = sorted(far, key=lambda k: (k & 1, -k)), sorted(near, key=lambda k: (k & 1, k))
+    order = [k for pair in zip(far_order, near_order) for k in pair] + far_order[len(near):]
 
     def cost(steps):
         return pl.CostEstimate(flops=steps, bytes_accessed=steps, transcendentals=0)

time: 117 us -> 112 us (0.957)
  waiting for transfers between devices: 36.3 us -> 31.6 us
    ppermute x28, waiting for transfers between devices: 36.3 us -> 31.6 us  [moved(): return lax.ppermute(value, 'src', [(i, i ^ k) for i in range(groups)])]
  transfers between devices with their start and end apart: 30 -> 30, of which waited for: 10 -> 9; matrix products, arithmetic and copies ran while one was open for 1% -> 1% of each run, Pallas kernels for 8% -> 9%
where the time goes in v2:
time: 112 us; the launch traced here: 111 us
  starting transfers between devices  56.2 us (50%)
  waiting for transfers between devices  31.6 us (28%)
  Pallas kernels  19.9 us (18%)
  local copies, waits for them, and re-layouts  3.39 us (3%)
    ppermute x28, starting transfers between devices, moved(): return lax.ppermute(value, 'src', [(i, i ^ k) for i in range(groups)])  56.1 us
    ppermute x28, waiting for transfers between devices, moved(): return lax.ppermute(value, 'src', [(i, i ^ k) for i in range(groups)])  31.6 us
    pallas_call x1, Pallas kernels, on_device(): pl.pallas_call(functools.partial(local_kernel, groups, halves, min(GROUP_...  8.76 us
    pallas_call x3, Pallas kernels, on_device(): pl.pallas_call(functools.partial(eval_kernel, part, [(k, half * some) for...  4.27 us
    pallas_call x1, Pallas kernels, on_device(): pl.pallas_call(functools.partial(tiles_kernel, part, bits, known), out_sh...  3.05 us
    unnamed x14, local copies, waits for them, and re-layouts  2.67 us
    pallas_call x2, Pallas kernels, on_device(): pl.pallas_call(functools.partial(remote_kernel, groups, half * some, part...  2.6 us
  transfers between devices with their start and end apart: 30, of which 9 were waited for; matrix products, arithmetic and copies ran while one was open for 1% of the time, Pallas kernels for 9%

profile of v2, /device:TPU:0, one launch (start us, length us, event | category | flops | bytes accessed | tf_op | source)
XLA Modules:
  0.0 111.4 jit_solution(3378919397173202612)
XLA Ops:
  0.0 8.8 %local.1 = (bf16[272,256]{1,0:T(8,128)(2,1)}, bf16[272,256]{1,0:T(8,128)(2,1)}, bf16[272,256]{1,0:T(8,128)(2,1)}, bf16[272,256]{1,0:T(8,128)(2,1)}, bf16[272,256...) custom-call(bf16[1,64]{1,0:T(2,128)(2,1)} %bitcast.2, ...), custom_call_target="tpu_custom_call" | custom-call | flops 192 | bytes 192 | tf_op jit(solution)/shard_map/local/pallas_call | solution.py:285
  8.8 5.1 %collective-permute-start = (bf16[272,256]{1,0:T(8,128)(2,1)}, bf16[272,256]{1,0:T(8,128)(2,1)S(1)}, u32[]{:S(2)}, u32[]{:S(2)}) collective-permute-start(bf16[272,256]{1,0:T(8,128)(2,1)} %get-tuple-element.40), channel_id=1, source_target_pairs={{0,12},{2,14},{4,8},{6,10},{8,4},{10,6},{12,0},{14,2},{1,13},{3,15... | collective-permute-start | bytes 417800 | tf_op jit(solution)/shard_map/ppermute | solution.py:283
  14.5 1.7 %collective-permute-start.4 = (bf16[256,256]{1,0:T(8,128)(2,1)}, bf16[256,256]{1,0:T(8,128)(2,1)S(1)}, u32[]{:S(2)}, u32[]{:S(2)}) collective-permute-start(bf16[256,256]{1,0:T(8,128)(2,1)} %get-tuple-element.47), channel_id=1, source_target_pairs={{0,2},{2,0},{4,6},{6,4},{8,10},{10,8},{12,14},{14,12},{1,3},{3,1},... | collective-permute-start | bytes 393224 | tf_op jit(solution)/shard_map/ppermute | solution.py:283
  16.6 4.3 %collective-permute-done.4.rest_1_ = bf16[256,256]{1,0:T(8,128)(2,1)S(1)} collective-permute-done((bf16[256,256]{1,0:T(8,128)(2,1)}, bf16[256,256]{1,0:T(8,128)(2,1)S(1)}, u32[]{:S(2)}, u32[]{:S(2)}) %collective-permute-start.4) | collective-permute-done | bytes 131104 | tf_op jit(solution)/shard_map/ppermute | solution.py:283
  20.9 2.3 %collective-permute-start.11 = (bf16[272,256]{1,0:T(8,128)(2,1)}, bf16[272,256]{1,0:T(8,128)(2,1)S(1)}, u32[]{:S(2)}, u32[]{:S(2)}) collective-permute-start(bf16[272,256]{1,0:T(8,128)(2,1)} %get-tuple-element.54), channel_id=1, source_target_pairs={{0,6},{2,4},{4,2},{6,0},{8,14},{10,12},{12,10},{14,8},{1,7},{3,5},... | collective-permute-start | bytes 417800 | tf_op jit(solution)/shard_map/ppermute | solution.py:283
  23.3 2.6 %collective-permute-start.12 = (bf16[272,256]{1,0:T(8,128)(2,1)}, bf16[272,256]{1,0:T(8,128)(2,1)S(1)}, u32[]{:S(2)}, u32[]{:S(2)}) collective-permute-start(bf16[272,256]{1,0:T(8,128)(2,1)} %get-tuple-element.55), channel_id=1, source_target_pairs={{0,10},{2,8},{4,14},{6,12},{8,2},{10,0},{12,6},{14,4},{1,11},{3,9}... | collective-permute-start | bytes 417800 | tf_op jit(solution)/shard_map/ppermute | solution.py:283
  25.8 1.3 %collective-permute-start.13 = (bf16[272,256]{1,0:T(8,128)(2,1)}, bf16[272,256]{1,0:T(8,128)(2,1)S(1)}, u32[]{:S(2)}, u32[]{:S(2)}) collective-permute-start(bf16[272,256]{1,0:T(8,128)(2,1)} %get-tuple-element.56), channel_id=1, source_target_pairs={{0,14},{2,12},{4,10},{6,8},{8,6},{10,4},{12,2},{14,0},{1,15},{3,13... | collective-permute-start | bytes 417800 | tf_op jit(solution)/shard_map/ppermute | solution.py:283
  27.2 1.6 %collective-permute-done.2.rest_4_ = bf16[272,256]{1,0:T(8,128)(2,1)S(1)} collective-permute-done((bf16[272,256]{1,0:T(8,128)(2,1)}, bf16[272,256]{1,0:T(8,128)(2,1)S(1)}, u32[]{:S(2)}, u32[]{:S(2)}) %collective-permute-start.2) | collective-permute-done | bytes 139296 | tf_op jit(solution)/shard_map/ppermute | solution.py:283
  28.8 4.5 %collective-permute-start.6 = (bf16[256,256]{1,0:T(8,128)(2,1)}, bf16[256,256]{1,0:T(8,128)(2,1)S(1)}, u32[]{:S(2)}, u32[]{:S(2)}) collective-permute-start(bf16[256,256]{1,0:T(8,128)(2,1)} %get-tuple-element.49), channel_id=1, source_target_pairs={{0,6},{2,4},{4,2},{6,0},{8,14},{10,12},{12,10},{14,8},{1,7},{3,5},... | collective-permute-start | bytes 393224 | tf_op jit(solution)/shard_map/ppermute | solution.py:283
  35.7 3.1 %remote_tiles.1 = (bf16[3,40,64,128]{3,2,1,0:T(8,128)(2,1)S(1)}, bf16[40,64,128]{2,1,0:T(8,128)(2,1)S(1)}) custom-call(bf16[5,64]{1,0:T(8,128)(2,1)S(1)} %concatenate.3.warp_ref, bf16[2,2,64,64]{3,2,1,0:T(8,128)(2,1)S(1)} %copy-done.1, f32[2,2,64,64]{3,2,1,0:T(8,128)S(1)} %copy-done), custom_call_target="tpu_custom_call" | custom-call | flops 128 | bytes 128 | tf_op jit(solution)/shard_map/remote_tiles/pallas_call | solution.py:314
  38.9 2.6 %collective-permute-start.8 = (bf16[256,256]{1,0:T(8,128)(2,1)}, bf16[256,256]{1,0:T(8,128)(2,1)S(1)}, u32[]{:S(2)}, u32[]{:S(2)}) collective-permute-start(bf16[256,256]{1,0:T(8,128)(2,1)} %get-tuple-element.51), channel_id=1, source_target_pairs={{0,10},{2,8},{4,14},{6,12},{8,2},{10,0},{12,6},{14,4},{1,11},{3,9}... | collective-permute-start | bytes 393224 | tf_op jit(solution)/shard_map/ppermute | solution.py:283
  41.4 2.3 %collective-permute-start.9 = (bf16[256,256]{1,0:T(8,128)(2,1)}, bf16[256,256]{1,0:T(8,128)(2,1)S(1)}, u32[]{:S(2)}, u32[]{:S(2)}) collective-permute-start(bf16[256,256]{1,0:T(8,128)(2,1)} %get-tuple-element.52), channel_id=1, source_target_pairs={{0,12},{2,14},{4,8},{6,10},{8,4},{10,6},{12,0},{14,2},{1,13},{3,15... | collective-permute-start | bytes 393224 | tf_op jit(solution)/shard_map/ppermute | solution.py:283
  43.7 2.8 %collective-permute-start.10 = (bf16[256,256]{1,0:T(8,128)(2,1)}, bf16[256,256]{1,0:T(8,128)(2,1)S(1)}, u32[]{:S(2)}, u32[]{:S(2)}) collective-permute-start(bf16[256,256]{1,0:T(8,128)(2,1)} %get-tuple-element.53), channel_id=1, source_target_pairs={{0,14},{2,12},{4,10},{6,8},{8,6},{10,4},{12,2},{14,0},{1,15},{3,13... | collective-permute-start | bytes 393224 | tf_op jit(solution)/shard_map/ppermute | solution.py:283
  48.7 4.7 %collective-permute-done.7.rest_4_ = bf16[256,256]{1,0:T(8,128)(2,1)S(1)} collective-permute-done((bf16[256,256]{1,0:T(8,128)(2,1)}, bf16[256,256]{1,0:T(8,128)(2,1)S(1)}, u32[]{:S(2)}, u32[]{:S(2)}) %collective-permute-start.7) | collective-permute-done | bytes 131104 | tf_op jit(solution)/shard_map/ppermute | solution.py:283
  53.5 4.1 %collective-permute-done.8.rest_5_ = bf16[256,256]{1,0:T(8,128)(2,1)S(1)} collective-permute-done((bf16[256,256]{1,0:T(8,128)(2,1)}, bf16[256,256]{1,0:T(8,128)(2,1)S(1)}, u32[]{:S(2)}, u32[]{:S(2)}) %collective-permute-start.8) | collective-permute-done | bytes 131104 | tf_op jit(solution)/shard_map/ppermute | solution.py:283
  57.6 1.4 %remote_1.1.own = bf16[32,64,256]{2,1,0:T(8,128)(2,1)S(1)} custom-call(bf16[3,40,64,128]{3,2,1,0:T(8,128)(2,1)S(1)} %get-tuple-element.45.tiles, bf16[2,2,64,64]{3,2,1,0:T(8,128)(2,1)S(1)} %copy-done.1, f32[2,2,64,64]{3,2,1,0:T(8,128)S(1)} %copy-done, bf16[256,256]{1,0:T(8,128)(2,1)S(1)} %copy-done.5, bf16[256,256]{1,0:T(8,128)(2,1)S(1)} %collective-permute-done.4.rest_1_, ...), custom_call_target="tpu_custom_call" | custom-call | flops 48 | bytes 48 | tf_op jit(solution)/shard_map/remote_1/pallas_call | solution.py:331
  59.7 2.8 %collective-permute-start.23 = (bf16[256,256]{1,0:T(8,128)(2,1)S(1)}, bf16[256,256]{1,0:T(8,128)(2,1)S(1)}, u32[]{:S(2)}, u32[]{:S(2)}) collective-permute-start(bf16[256,256]{1,0:T(8,128)(2,1)S(1)} %get-tuple-element.66), channel_id=1, source_target_pairs={{0,12},{2,14},{4,8},{6,10},{8,4},{10,6},{12,0},{14,2},{1,13},{3,15... | collective-permute-start | bytes 393224 | tf_op jit(solution)/shard_map/ppermute | solution.py:283
  62.6 3.2 %collective-permute-start.24 = (bf16[256,256]{1,0:T(8,128)(2,1)S(1)}, bf16[256,256]{1,0:T(8,128)(2,1)S(1)}, u32[]{:S(2)}, u32[]{:S(2)}) collective-permute-start(bf16[256,256]{1,0:T(8,128)(2,1)S(1)} %get-tuple-element.67), channel_id=1, source_target_pairs={{0,4},{2,6},{4,0},{6,2},{8,12},{10,14},{12,8},{14,10},{1,5},{3,7},... | collective-permute-start | bytes 393224 | tf_op jit(solution)/shard_map/ppermute | solution.py:283
  66.2 3.4 %collective-permute-start.27 = (bf16[256,256]{1,0:T(8,128)(2,1)S(1)}, bf16[256,256]{1,0:T(8,128)(2,1)S(1)}, u32[]{:S(2)}, u32[]{:S(2)}) collective-permute-start(bf16[256,256]{1,0:T(8,128)(2,1)S(1)} %get-tuple-element.70), channel_id=1, source_target_pairs={{0,14},{2,12},{4,10},{6,8},{8,6},{10,4},{12,2},{14,0},{1,15},{3,13... | collective-permute-start | bytes 393224 | tf_op jit(solution)/shard_map/ppermute | solution.py:283
  71.2 2.1 %collective-permute-start.29 = (bf16[256,256]{1,0:T(8,128)(2,1)S(1)}, bf16[256,256]{1,0:T(8,128)(2,1)S(1)}, u32[]{:S(2)}, u32[]{:S(2)}) collective-permute-start(bf16[256,256]{1,0:T(8,128)(2,1)S(1)} %get-tuple-element.72), channel_id=1, source_target_pairs={{0,10},{2,8},{4,14},{6,12},{8,2},{10,0},{12,6},{14,4},{1,11},{3,9}... | collective-permute-start | bytes 393224 | tf_op jit(solution)/shard_map/ppermute | solution.py:283
  73.3 5.7 %collective-permute-done.25.rest_3_ = bf16[256,256]{1,0:T(8,128)(2,1)S(1)} collective-permute-done((bf16[256,256]{1,0:T(8,128)(2,1)S(1)}, bf16[256,256]{1,0:T(8,128)(2,1)S(1)}, u32[]{:S(2)}, u32[]{:S(2)}) %collective-permute-start.25) | collective-permute-done | bytes 131104 | tf_op jit(solution)/shard_map/ppermute | solution.py:283
  79.0 3.2 %collective-permute-start.18 = (bf16[256,256]{1,0:T(8,128)(2,1)S(1)}, bf16[256,256]{1,0:T(8,128)(2,1)S(1)}, u32[]{:S(2)}, u32[]{:S(2)}) collective-permute-start(bf16[256,256]{1,0:T(8,128)(2,1)S(1)} %get-tuple-element.61), channel_id=1, source_target_pairs={{0,12},{2,14},{4,8},{6,10},{8,4},{10,6},{12,0},{14,2},{1,13},{3,15... | collective-permute-start | bytes 393224 | tf_op jit(solution)/shard_map/ppermute | solution.py:283
  82.4 8.3 %collective-permute-start.20 = (bf16[256,256]{1,0:T(8,128)(2,1)S(1)}, bf16[256,256]{1,0:T(8,128)(2,1)S(1)}, u32[]{:S(2)}, u32[]{:S(2)}) collective-permute-start(bf16[256,256]{1,0:T(8,128)(2,1)S(1)} %get-tuple-element.63), channel_id=1, source_target_pairs={{0,8},{2,10},{4,12},{6,14},{8,0},{10,2},{12,4},{14,6},{1,9},{3,11}... | collective-permute-start | bytes 393224 | tf_op jit(solution)/shard_map/ppermute | solution.py:283
  90.7 5.4 %collective-permute-done.29.rest_7_ = bf16[256,256]{1,0:T(8,128)(2,1)S(1)} collective-permute-done((bf16[256,256]{1,0:T(8,128)(2,1)S(1)}, bf16[256,256]{1,0:T(8,128)(2,1)S(1)}, u32[]{:S(2)}, u32[]{:S(2)}) %collective-permute-start.29) | collective-permute-done | bytes 131104 | tf_op jit(solution)/shard_map/ppermute | solution.py:283
  96.1 1.6 %collective-permute-start.21 = (bf16[256,256]{1,0:T(8,128)(2,1)S(1)}, bf16[256,256]{1,0:T(8,128)(2,1)S(1)}, u32[]{:S(2)}, u32[]{:S(2)}) collective-permute-start(bf16[256,256]{1,0:T(8,128)(2,1)S(1)} %get-tuple-element.64), channel_id=1, source_target_pairs={{0,2},{2,0},{4,6},{6,4},{8,10},{10,8},{12,14},{14,12},{1,3},{3,1},... | collective-permute-start | bytes 393224 | tf_op jit(solution)/shard_map/ppermute | solution.py:283
  97.7 1.8 %collective-permute-start.16 = (bf16[256,256]{1,0:T(8,128)(2,1)S(1)}, bf16[256,256]{1,0:T(8,128)(2,1)S(1)}, u32[]{:S(2)}, u32[]{:S(2)}) collective-permute-start(bf16[256,256]{1,0:T(8,128)(2,1)S(1)} %get-tuple-element.58), channel_id=1, source_target_pairs={{0,6},{2,4},{4,2},{6,0},{8,14},{10,12},{12,10},{14,8},{1,7},{3,5},... | collective-permute-start | bytes 393224 | tf_op jit(solution)/shard_map/ppermute | solution.py:283
  99.5 1.9 %collective-permute-start.17 = (bf16[256,256]{1,0:T(8,128)(2,1)S(1)}, bf16[256,256]{1,0:T(8,128)(2,1)S(1)}, u32[]{:S(2)}, u32[]{:S(2)}) collective-permute-start(bf16[256,256]{1,0:T(8,128)(2,1)S(1)} %get-tuple-element.59), channel_id=1, source_target_pairs={{0,10},{2,8},{4,14},{6,12},{8,2},{10,0},{12,6},{14,4},{1,11},{3,9}... | collective-permute-start | bytes 393224 | tf_op jit(solution)/shard_map/ppermute | solution.py:283
  101.4 1.7 %eval_0.1.rest_5_ = f32[8,8,64,256]{3,2,1,0:T(8,128)} custom-call(bf16[1,64]{1,0:T(2,128)(2,1)S(1)} %bitcast.3, bf16[64,64]{1,0:T(8,128)(2,1)S(1)} %copy-done.3, f32[64,64]{1,0:T(8,128)S(1)} %copy-done.2, bf16[256,256]{1,0:T(8,128)(2,1)S(1)} %get-tuple-element.65.rest_0_, bf16[256,256]{1,0:T(8,128)(2,1)S(1)} %collective-permute-done.23.rest_1_, ...), custom_call_target="tpu_custom_call" | custom-call | flops 8 | bytes 8 | tf_op jit(solution)/shard_map/eval_0/pallas_call | solution.py:365
  103.0 2.0 %collective-permute-done.20.rest_3_ = bf16[256,256]{1,0:T(8,128)(2,1)S(1)} collective-permute-done((bf16[256,256]{1,0:T(8,128)(2,1)S(1)}, bf16[256,256]{1,0:T(8,128)(2,1)S(1)}, u32[]{:S(2)}, u32[]{:S(2)}) %collective-permute-start.20) | collective-permute-done | bytes 131104 | tf_op jit(solution)/shard_map/ppermute | solution.py:283
  105.1 1.4 %eval_1.1.rest_3_ = f32[8,8,64,256]{3,2,1,0:T(8,128)} custom-call(bf16[1,64]{1,0:T(2,128)(2,1)S(1)} %bitcast.4, bf16[64,64]{1,0:T(8,128)(2,1)S(1)} %copy-done.3, f32[64,64]{1,0:T(8,128)S(1)} %copy-done.2, bf16[256,256]{1,0:T(8,128)(2,1)S(1)} %get-tuple-element.60.rest_0_, ...), custom_call_target="tpu_custom_call", output_to_operand_aliasing={{}: (8, {})} | custom-call | flops 5 | bytes 5 | tf_op jit(solution)/shard_map/eval_1/pallas_call | solution.py:365
  106.5 1.8 %collective-permute-done.16.rest_1_ = bf16[256,256]{1,0:T(8,128)(2,1)S(1)} collective-permute-done((bf16[256,256]{1,0:T(8,128)(2,1)S(1)}, bf16[256,256]{1,0:T(8,128)(2,1)S(1)}, u32[]{:S(2)}, u32[]{:S(2)}) %collective-permute-start.16) | collective-permute-done | bytes 131104 | tf_op jit(solution)/shard_map/ppermute | solution.py:283
  108.3 1.7 %collective-permute-done.17.rest_2_ = bf16[256,256]{1,0:T(8,128)(2,1)S(1)} collective-permute-done((bf16[256,256]{1,0:T(8,128)(2,1)S(1)}, bf16[256,256]{1,0:T(8,128)(2,1)S(1)}, u32[]{:S(2)}, u32[]{:S(2)}) %collective-permute-start.17) | collective-permute-done | bytes 131104 | tf_op jit(solution)/shard_map/ppermute | solution.py:283
  (57 shorter events, 9.9 us)
Async XLA Ops:
  8.8 14.5 %collective-permute-start = (bf16[272,256]{1,0:T(8,128)(2,1)}, bf16[272,256]{1,0:T(8,128)(2,1)S(1)}, u32[]{:S(2)}, u32[]{:S(2)}) collective-permute-start(bf16[272,256]{1,0:T(8,128)(2,1)} %get-tuple-element.40), channel_id=1, source_target_pairs={{0,12},{2,14},{4,8},{6,10},{8,4},{10,6},{12,0},{14,2},{1,13},{3,15... | collective-permute-start | bytes 417800 | tf_op jit(solution)/shard_map/ppermute | solution.py:283
  13.9 12.0 %collective-permute-start.1 = (bf16[272,256]{1,0:T(8,128)(2,1)}, bf16[272,256]{1,0:T(8,128)(2,1)S(1)}, u32[]{:S(2)}, u32[]{:S(2)}) collective-permute-start(bf16[272,256]{1,0:T(8,128)(2,1)} %get-tuple-element.41), channel_id=1, source_target_pairs={{0,4},{2,6},{4,0},{6,2},{8,12},{10,14},{12,8},{14,10},{1,5},{3,7},... | collective-permute-start | bytes 417800 | tf_op jit(solution)/shard_map/ppermute | solution.py:283
  13.9 14.9 %collective-permute-start.2 = (bf16[272,256]{1,0:T(8,128)(2,1)}, bf16[272,256]{1,0:T(8,128)(2,1)S(1)}, u32[]{:S(2)}, u32[]{:S(2)}) collective-permute-start(bf16[272,256]{1,0:T(8,128)(2,1)} %get-tuple-element.42), channel_id=1, source_target_pairs={{0,8},{2,10},{4,12},{6,14},{8,0},{10,2},{12,4},{14,6},{1,9},{3,11}... | collective-permute-start | bytes 417800 | tf_op jit(solution)/shard_map/ppermute | solution.py:283
  14.5 6.4 %collective-permute-start.4 = (bf16[256,256]{1,0:T(8,128)(2,1)}, bf16[256,256]{1,0:T(8,128)(2,1)S(1)}, u32[]{:S(2)}, u32[]{:S(2)}) collective-permute-start(bf16[256,256]{1,0:T(8,128)(2,1)} %get-tuple-element.47), channel_id=1, source_target_pairs={{0,2},{2,0},{4,6},{6,4},{8,10},{10,8},{12,14},{14,12},{1,3},{3,1},... | collective-permute-start | bytes 393224 | tf_op jit(solution)/shard_map/ppermute | solution.py:283
  16.2 12.6 %collective-permute-start.3 = (bf16[272,256]{1,0:T(8,128)(2,1)}, bf16[272,256]{1,0:T(8,128)(2,1)S(1)}, u32[]{:S(2)}, u32[]{:S(2)}) collective-permute-start(bf16[272,256]{1,0:T(8,128)(2,1)} %get-tuple-element.43), channel_id=1, source_target_pairs={{0,2},{2,0},{4,6},{6,4},{8,10},{10,8},{12,14},{14,12},{1,3},{3,1},... | collective-permute-start | bytes 417800 | tf_op jit(solution)/shard_map/ppermute | solution.py:283
  20.9 18.0 %collective-permute-start.11 = (bf16[272,256]{1,0:T(8,128)(2,1)}, bf16[272,256]{1,0:T(8,128)(2,1)S(1)}, u32[]{:S(2)}, u32[]{:S(2)}) collective-permute-start(bf16[272,256]{1,0:T(8,128)(2,1)} %get-tuple-element.54), channel_id=1, source_target_pairs={{0,6},{2,4},{4,2},{6,0},{8,14},{10,12},{12,10},{14,8},{1,7},{3,5},... | collective-permute-start | bytes 417800 | tf_op jit(solution)/shard_map/ppermute | solution.py:283
  23.3 18.2 %collective-permute-start.12 = (bf16[272,256]{1,0:T(8,128)(2,1)}, bf16[272,256]{1,0:T(8,128)(2,1)S(1)}, u32[]{:S(2)}, u32[]{:S(2)}) collective-permute-start(bf16[272,256]{1,0:T(8,128)(2,1)} %get-tuple-element.55), channel_id=1, source_target_pairs={{0,10},{2,8},{4,14},{6,12},{8,2},{10,0},{12,6},{14,4},{1,11},{3,9}... | collective-permute-start | bytes 417800 | tf_op jit(solution)/shard_map/ppermute | solution.py:283
  25.8 17.9 %collective-permute-start.13 = (bf16[272,256]{1,0:T(8,128)(2,1)}, bf16[272,256]{1,0:T(8,128)(2,1)S(1)}, u32[]{:S(2)}, u32[]{:S(2)}) collective-permute-start(bf16[272,256]{1,0:T(8,128)(2,1)} %get-tuple-element.56), channel_id=1, source_target_pairs={{0,14},{2,12},{4,10},{6,8},{8,6},{10,4},{12,2},{14,0},{1,15},{3,13... | collective-permute-start | bytes 417800 | tf_op jit(solution)/shard_map/ppermute | solution.py:283
  28.8 10.0 %collective-permute-start.5 = (bf16[256,256]{1,0:T(8,128)(2,1)}, bf16[256,256]{1,0:T(8,128)(2,1)S(1)}, u32[]{:S(2)}, u32[]{:S(2)}) collective-permute-start(bf16[256,256]{1,0:T(8,128)(2,1)} %get-tuple-element.48), channel_id=1, source_target_pairs={{0,4},{2,6},{4,0},{6,2},{8,12},{10,14},{12,8},{14,10},{1,5},{3,7},... | collective-permute-start | bytes 393224 | tf_op jit(solution)/shard_map/ppermute | solution.py:283
  28.8 19.9 %collective-permute-start.6 = (bf16[256,256]{1,0:T(8,128)(2,1)}, bf16[256,256]{1,0:T(8,128)(2,1)S(1)}, u32[]{:S(2)}, u32[]{:S(2)}) collective-permute-start(bf16[256,256]{1,0:T(8,128)(2,1)} %get-tuple-element.49), channel_id=1, source_target_pairs={{0,6},{2,4},{4,2},{6,0},{8,14},{10,12},{12,10},{14,8},{1,7},{3,5},... | collective-permute-start | bytes 393224 | tf_op jit(solution)/shard_map/ppermute | solution.py:283
  38.8 14.7 %collective-permute-start.7 = (bf16[256,256]{1,0:T(8,128)(2,1)}, bf16[256,256]{1,0:T(8,128)(2,1)S(1)}, u32[]{:S(2)}, u32[]{:S(2)}) collective-permute-start(bf16[256,256]{1,0:T(8,128)(2,1)} %get-tuple-element.50), channel_id=1, source_target_pairs={{0,8},{2,10},{4,12},{6,14},{8,0},{10,2},{12,4},{14,6},{1,9},{3,11}... | collective-permute-start | bytes 393224 | tf_op jit(solution)/shard_map/ppermute | solution.py:283
  38.9 18.7 %collective-permute-start.8 = (bf16[256,256]{1,0:T(8,128)(2,1)}, bf16[256,256]{1,0:T(8,128)(2,1)S(1)}, u32[]{:S(2)}, u32[]{:S(2)}) collective-permute-start(bf16[256,256]{1,0:T(8,128)(2,1)} %get-tuple-element.51), channel_id=1, source_target_pairs={{0,10},{2,8},{4,14},{6,12},{8,2},{10,0},{12,6},{14,4},{1,11},{3,9}... | collective-permute-start | bytes 393224 | tf_op jit(solution)/shard_map/ppermute | solution.py:283
  41.4 16.2 %collective-permute-start.9 = (bf16[256,256]{1,0:T(8,128)(2,1)}, bf16[256,256]{1,0:T(8,128)(2,1)S(1)}, u32[]{:S(2)}, u32[]{:S(2)}) collective-permute-start(bf16[256,256]{1,0:T(8,128)(2,1)} %get-tuple-element.52), channel_id=1, source_target_pairs={{0,12},{2,14},{4,8},{6,10},{8,4},{10,6},{12,0},{14,2},{1,13},{3,15... | collective-permute-start | bytes 393224 | tf_op jit(solution)/shard_map/ppermute | solution.py:283
  43.7 13.9 %collective-permute-start.10 = (bf16[256,256]{1,0:T(8,128)(2,1)}, bf16[256,256]{1,0:T(8,128)(2,1)S(1)}, u32[]{:S(2)}, u32[]{:S(2)}) collective-permute-start(bf16[256,256]{1,0:T(8,128)(2,1)} %get-tuple-element.53), channel_id=1, source_target_pairs={{0,14},{2,12},{4,10},{6,8},{8,6},{10,4},{12,2},{14,0},{1,15},{3,13... | collective-permute-start | bytes 393224 | tf_op jit(solution)/shard_map/ppermute | solution.py:283
  48.6 10.5 %collective-permute-start.22 = (bf16[32,64,256]{2,1,0:T(8,128)(2,1)S(1)}, bf16[32,64,256]{2,1,0:T(8,128)(2,1)S(1)}, u32[]{:S(2)}, u32[]{:S(2)}) collective-permute-start(bf16[32,64,256]{2,1,0:T(8,128)(2,1)S(1)} %remote_0.1.own), channel_id=1, source_target_pairs={{0,1},{1,0},{2,3},{3,2},{4,5},{5,4},{6,7},{7,6},{8,9},{9,8},{10,11... | collective-permute-start | bytes 3145736 | tf_op jit(solution)/shard_map/ppermute | solution.py:341
  59.0 42.4 %copy-start.2 = (f32[64,64]{1,0:T(8,128)S(1)}, f32[64,64]{1,0:T(8,128)}, u32[]{:S(2)}) copy-start(f32[64,64]{1,0:T(8,128)} %omega_ref.15) | copy-start | bytes 49156
  59.0 42.3 %copy-start.3 = (bf16[64,64]{1,0:T(8,128)(2,1)S(1)}, bf16[64,64]{1,0:T(8,128)(2,1)}, u32[]{:S(2)}) copy-start(bf16[64,64]{1,0:T(8,128)(2,1)} %interp_ref.15) | copy-start | bytes 24580
  59.0 7.1 %collective-permute-start.14 = (bf16[32,64,256]{2,1,0:T(8,128)(2,1)S(1)}, bf16[32,64,256]{2,1,0:T(8,128)(2,1)S(1)}, u32[]{:S(2)}, u32[]{:S(2)}) collective-permute-start(bf16[32,64,256]{2,1,0:T(8,128)(2,1)S(1)} %remote_1.1.own), channel_id=1, source_target_pairs={{0,1},{1,0},{2,3},{3,2},{4,5},{5,4},{6,7},{7,6},{8,9},{9,8},{10,11... | collective-permute-start | bytes 3145736 | tf_op jit(solution)/shard_map/ppermute | solution.py:341
  59.7 10.4 %collective-permute-start.23 = (bf16[256,256]{1,0:T(8,128)(2,1)S(1)}, bf16[256,256]{1,0:T(8,128)(2,1)S(1)}, u32[]{:S(2)}, u32[]{:S(2)}) collective-permute-start(bf16[256,256]{1,0:T(8,128)(2,1)S(1)} %get-tuple-element.66), channel_id=1, source_target_pairs={{0,12},{2,14},{4,8},{6,10},{8,4},{10,6},{12,0},{14,2},{1,13},{3,15... | collective-permute-start | bytes 393224 | tf_op jit(solution)/shard_map/ppermute | solution.py:283
  62.6 8.7 %collective-permute-start.24 = (bf16[256,256]{1,0:T(8,128)(2,1)S(1)}, bf16[256,256]{1,0:T(8,128)(2,1)S(1)}, u32[]{:S(2)}, u32[]{:S(2)}) collective-permute-start(bf16[256,256]{1,0:T(8,128)(2,1)S(1)} %get-tuple-element.67), channel_id=1, source_target_pairs={{0,4},{2,6},{4,0},{6,2},{8,12},{10,14},{12,8},{14,10},{1,5},{3,7},... | collective-permute-start | bytes 393224 | tf_op jit(solution)/shard_map/ppermute | solution.py:283
  65.8 13.2 %collective-permute-start.25 = (bf16[256,256]{1,0:T(8,128)(2,1)S(1)}, bf16[256,256]{1,0:T(8,128)(2,1)S(1)}, u32[]{:S(2)}, u32[]{:S(2)}) collective-permute-start(bf16[256,256]{1,0:T(8,128)(2,1)S(1)} %get-tuple-element.68), channel_id=1, source_target_pairs={{0,8},{2,10},{4,12},{6,14},{8,0},{10,2},{12,4},{14,6},{1,9},{3,11}... | collective-permute-start | bytes 393224 | tf_op jit(solution)/shard_map/ppermute | solution.py:283
  65.9 16.4 %collective-permute-start.26 = (bf16[256,256]{1,0:T(8,128)(2,1)S(1)}, bf16[256,256]{1,0:T(8,128)(2,1)S(1)}, u32[]{:S(2)}, u32[]{:S(2)}) collective-permute-start(bf16[256,256]{1,0:T(8,128)(2,1)S(1)} %get-tuple-element.69), channel_id=1, source_target_pairs={{0,2},{2,0},{4,6},{6,4},{8,10},{10,8},{12,14},{14,12},{1,3},{3,1},... | collective-permute-start | bytes 393224 | tf_op jit(solution)/shard_map/ppermute | solution.py:283
  66.2 16.1 %collective-permute-start.27 = (bf16[256,256]{1,0:T(8,128)(2,1)S(1)}, bf16[256,256]{1,0:T(8,128)(2,1)S(1)}, u32[]{:S(2)}, u32[]{:S(2)}) collective-permute-start(bf16[256,256]{1,0:T(8,128)(2,1)S(1)} %get-tuple-element.70), channel_id=1, source_target_pairs={{0,14},{2,12},{4,10},{6,8},{8,6},{10,4},{12,2},{14,0},{1,15},{3,13... | collective-permute-start | bytes 393224 | tf_op jit(solution)/shard_map/ppermute | solution.py:283
  70.2 12.2 %collective-permute-start.28 = (bf16[256,256]{1,0:T(8,128)(2,1)S(1)}, bf16[256,256]{1,0:T(8,128)(2,1)S(1)}, u32[]{:S(2)}, u32[]{:S(2)}) collective-permute-start(bf16[256,256]{1,0:T(8,128)(2,1)S(1)} %get-tuple-element.71), channel_id=1, source_target_pairs={{0,6},{2,4},{4,2},{6,0},{8,14},{10,12},{12,10},{14,8},{1,7},{3,5},... | collective-permute-start | bytes 393224 | tf_op jit(solution)/shard_map/ppermute | solution.py:283
  71.2 24.8 %collective-permute-start.29 = (bf16[256,256]{1,0:T(8,128)(2,1)S(1)}, bf16[256,256]{1,0:T(8,128)(2,1)S(1)}, u32[]{:S(2)}, u32[]{:S(2)}) collective-permute-start(bf16[256,256]{1,0:T(8,128)(2,1)S(1)} %get-tuple-element.72), channel_id=1, source_target_pairs={{0,10},{2,8},{4,14},{6,12},{8,2},{10,0},{12,6},{14,4},{1,11},{3,9}... | collective-permute-start | bytes 393224 | tf_op jit(solution)/shard_map/ppermute | solution.py:283
  79.0 18.7 %collective-permute-start.18 = (bf16[256,256]{1,0:T(8,128)(2,1)S(1)}, bf16[256,256]{1,0:T(8,128)(2,1)S(1)}, u32[]{:S(2)}, u32[]{:S(2)}) collective-permute-start(bf16[256,256]{1,0:T(8,128)(2,1)S(1)} %get-tuple-element.61), channel_id=1, source_target_pairs={{0,12},{2,14},{4,8},{6,10},{8,4},{10,6},{12,0},{14,2},{1,13},{3,15... | collective-permute-start | bytes 393224 | tf_op jit(solution)/shard_map/ppermute | solution.py:283
  82.2 17.2 %collective-permute-start.19 = (bf16[256,256]{1,0:T(8,128)(2,1)S(1)}, bf16[256,256]{1,0:T(8,128)(2,1)S(1)}, u32[]{:S(2)}, u32[]{:S(2)}) collective-permute-start(bf16[256,256]{1,0:T(8,128)(2,1)S(1)} %get-tuple-element.62), channel_id=1, source_target_pairs={{0,4},{2,6},{4,0},{6,2},{8,12},{10,14},{12,8},{14,10},{1,5},{3,7},... | collective-permute-start | bytes 393224 | tf_op jit(solution)/shard_map/ppermute | solution.py:283
  82.2 24.2 %collective-permute-start.15 = (bf16[256,256]{1,0:T(8,128)(2,1)S(1)}, bf16[256,256]{1,0:T(8,128)(2,1)S(1)}, u32[]{:S(2)}, u32[]{:S(2)}) collective-permute-start(bf16[256,256]{1,0:T(8,128)(2,1)S(1)} %get-tuple-element.57), channel_id=1, source_target_pairs={{0,14},{2,12},{4,10},{6,8},{8,6},{10,4},{12,2},{14,0},{1,15},{3,13... | collective-permute-start | bytes 393224 | tf_op jit(solution)/shard_map/ppermute | solution.py:283
  82.4 22.7 %collective-permute-start.20 = (bf16[256,256]{1,0:T(8,128)(2,1)S(1)}, bf16[256,256]{1,0:T(8,128)(2,1)S(1)}, u32[]{:S(2)}, u32[]{:S(2)}) collective-permute-start(bf16[256,256]{1,0:T(8,128)(2,1)S(1)} %get-tuple-element.63), channel_id=1, source_target_pairs={{0,8},{2,10},{4,12},{6,14},{8,0},{10,2},{12,4},{14,6},{1,9},{3,11}... | collective-permute-start | bytes 393224 | tf_op jit(solution)/shard_map/ppermute | solution.py:283
  96.1 9.0 %collective-permute-start.21 = (bf16[256,256]{1,0:T(8,128)(2,1)S(1)}, bf16[256,256]{1,0:T(8,128)(2,1)S(1)}, u32[]{:S(2)}, u32[]{:S(2)}) collective-permute-start(bf16[256,256]{1,0:T(8,128)(2,1)S(1)} %get-tuple-element.64), channel_id=1, source_target_pairs={{0,2},{2,0},{4,6},{6,4},{8,10},{10,8},{12,14},{14,12},{1,3},{3,1},... | collective-permute-start | bytes 393224 | tf_op jit(solution)/shard_map/ppermute | solution.py:283
  97.7 10.6 %collective-permute-start.16 = (bf16[256,256]{1,0:T(8,128)(2,1)S(1)}, bf16[256,256]{1,0:T(8,128)(2,1)S(1)}, u32[]{:S(2)}, u32[]{:S(2)}) collective-permute-start(bf16[256,256]{1,0:T(8,128)(2,1)S(1)} %get-tuple-element.58), channel_id=1, source_target_pairs={{0,6},{2,4},{4,2},{6,0},{8,14},{10,12},{12,10},{14,8},{1,7},{3,5},... | collective-permute-start | bytes 393224 | tf_op jit(solution)/shard_map/ppermute | solution.py:283
  99.5 10.6 %collective-permute-start.17 = (bf16[256,256]{1,0:T(8,128)(2,1)S(1)}, bf16[256,256]{1,0:T(8,128)(2,1)S(1)}, u32[]{:S(2)}, u32[]{:S(2)}) collective-permute-start(bf16[256,256]{1,0:T(8,128)(2,1)S(1)} %get-tuple-element.59), channel_id=1, source_target_pairs={{0,10},{2,8},{4,14},{6,12},{8,2},{10,0},{12,6},{14,4},{1,11},{3,9}... | collective-permute-start | bytes 393224 | tf_op jit(solution)/shard_map/ppermute | solution.py:283
  (5 other events, 66.9 us)

commit v3 on v2

--- a/solution.py
+++ b/solution.py
@@ -270,7 +270,7 @@
     long_block = jax.ShapeDtypeStruct((some * rank + WARP_ROWS, width), bf16)
     both_tables = [pltpu.VMEM((2, 2 * rank, 2 * rank), f32)] * 2
     far, near = list(range(groups // 2, groups)), list(range(1, groups // 2))
-    far_order, near_order = sorted(far, key=lambda k: (k & 1, -k)), sorted(near, key=lambda k: (k & 1, k))
+    far_order, near_order = sorted(far, key=lambda k: (k & 1, k if k & 1 else -k)), sorted(near, key=lambda k: (k & 1, k))
     order = [k for pair in zip(far_order, near_order) for k in pair] + far_order[len(near):]
 
     def cost(steps):

time: 112 us -> 111 us (level)
  waiting for transfers between devices: 31.6 us -> 27.1 us
  starting transfers between devices: 56.2 us -> 59.9 us
    ppermute x28, waiting for transfers between devices: 31.6 us -> 27.1 us  [moved(): return lax.ppermute(value, 'src', [(i, i ^ k) for i in range(groups)])]
    ppermute x28, starting transfers between devices: 56.1 us -> 59.7 us  [moved(): return lax.ppermute(value, 'src', [(i, i ^ k) for i in range(groups)])]
  transfers between devices with their start and end apart: 30 -> 30, of which waited for: 9 -> 8; matrix products, arithmetic and copies ran while one was open for 1% -> 1% of each run, Pallas kernels for 9% -> 9%
where the time goes in v3:
time: 111 us
  starting transfers between devices  59.9 us (54%)
  waiting for transfers between devices  27.1 us (24%)
  Pallas kernels  19.9 us (18%)
  local copies, waits for them, and re-layouts  3.39 us (3%)
    ppermute x28, starting transfers between devices, moved(): return lax.ppermute(value, 'src', [(i, i ^ k) for i in range(groups)])  59.7 us
    ppermute x28, waiting for transfers between devices, moved(): return lax.ppermute(value, 'src', [(i, i ^ k) for i in range(groups)])  27.1 us
    pallas_call x1, Pallas kernels, on_device(): pl.pallas_call(functools.partial(local_kernel, groups, halves, min(GROUP_...  8.76 us
    pallas_call x3, Pallas kernels, on_device(): pl.pallas_call(functools.partial(eval_kernel, part, [(k, half * some) for...  4.27 us
    pallas_call x1, Pallas kernels, on_device(): pl.pallas_call(functools.partial(tiles_kernel, part, bits, known), out_sh...  3.05 us
    unnamed x14, local copies, waits for them, and re-layouts  2.67 us
    pallas_call x2, Pallas kernels, on_device(): pl.pallas_call(functools.partial(remote_kernel, groups, half * some, part...  2.6 us
  transfers between devices with their start and end apart: 30, of which 8 were waited for; matrix products, arithmetic and copies ran while one was open for 1% of the time, Pallas kernels for 9%

profile of v3, /device:TPU:0, one launch (start us, length us, event | category | flops | bytes accessed | tf_op | source)
XLA Modules:
  0.0 110.6 jit_solution(11236592684406527458)
XLA Ops:
  0.0 8.8 %local.1 = (bf16[272,256]{1,0:T(8,128)(2,1)}, bf16[272,256]{1,0:T(8,128)(2,1)}, bf16[272,256]{1,0:T(8,128)(2,1)}, bf16[272,256]{1,0:T(8,128)(2,1)}, bf16[272,256...) custom-call(bf16[1,64]{1,0:T(2,128)(2,1)} %bitcast.2, ...), custom_call_target="tpu_custom_call" | custom-call | flops 192 | bytes 192 | tf_op jit(solution)/shard_map/local/pallas_call | solution.py:285
  8.8 5.1 %collective-permute-start = (bf16[272,256]{1,0:T(8,128)(2,1)}, bf16[272,256]{1,0:T(8,128)(2,1)S(1)}, u32[]{:S(2)}, u32[]{:S(2)}) collective-permute-start(bf16[272,256]{1,0:T(8,128)(2,1)} %get-tuple-element.40), channel_id=1, source_target_pairs={{0,12},{2,14},{4,8},{6,10},{8,4},{10,6},{12,0},{14,2},{1,13},{3,15... | collective-permute-start | bytes 417800 | tf_op jit(solution)/shard_map/ppermute | solution.py:283
  14.5 1.7 %collective-permute-start.4 = (bf16[256,256]{1,0:T(8,128)(2,1)}, bf16[256,256]{1,0:T(8,128)(2,1)S(1)}, u32[]{:S(2)}, u32[]{:S(2)}) collective-permute-start(bf16[256,256]{1,0:T(8,128)(2,1)} %get-tuple-element.47), channel_id=1, source_target_pairs={{0,2},{2,0},{4,6},{6,4},{8,10},{10,8},{12,14},{14,12},{1,3},{3,1},... | collective-permute-start | bytes 393224 | tf_op jit(solution)/shard_map/ppermute | solution.py:283
  16.6 4.3 %collective-permute-done.4.rest_1_ = bf16[256,256]{1,0:T(8,128)(2,1)S(1)} collective-permute-done((bf16[256,256]{1,0:T(8,128)(2,1)}, bf16[256,256]{1,0:T(8,128)(2,1)S(1)}, u32[]{:S(2)}, u32[]{:S(2)}) %collective-permute-start.4) | collective-permute-done | bytes 131104 | tf_op jit(solution)/shard_map/ppermute | solution.py:283
  20.9 2.3 %collective-permute-start.11 = (bf16[272,256]{1,0:T(8,128)(2,1)}, bf16[272,256]{1,0:T(8,128)(2,1)S(1)}, u32[]{:S(2)}, u32[]{:S(2)}) collective-permute-start(bf16[272,256]{1,0:T(8,128)(2,1)} %get-tuple-element.54), channel_id=1, source_target_pairs={{0,6},{2,4},{4,2},{6,0},{8,14},{10,12},{12,10},{14,8},{1,7},{3,5},... | collective-permute-start | bytes 417800 | tf_op jit(solution)/shard_map/ppermute | solution.py:283
  23.3 2.6 %collective-permute-start.12 = (bf16[272,256]{1,0:T(8,128)(2,1)}, bf16[272,256]{1,0:T(8,128)(2,1)S(1)}, u32[]{:S(2)}, u32[]{:S(2)}) collective-permute-start(bf16[272,256]{1,0:T(8,128)(2,1)} %get-tuple-element.55), channel_id=1, source_target_pairs={{0,10},{2,8},{4,14},{6,12},{8,2},{10,0},{12,6},{14,4},{1,11},{3,9}... | collective-permute-start | bytes 417800 | tf_op jit(solution)/shard_map/ppermute | solution.py:283
  25.8 1.3 %collective-permute-start.13 = (bf16[272,256]{1,0:T(8,128)(2,1)}, bf16[272,256]{1,0:T(8,128)(2,1)S(1)}, u32[]{:S(2)}, u32[]{:S(2)}) collective-permute-start(bf16[272,256]{1,0:T(8,128)(2,1)} %get-tuple-element.56), channel_id=1, source_target_pairs={{0,14},{2,12},{4,10},{6,8},{8,6},{10,4},{12,2},{14,0},{1,15},{3,13... | collective-permute-start | bytes 417800 | tf_op jit(solution)/shard_map/ppermute | solution.py:283
  27.2 1.6 %collective-permute-done.2.rest_4_ = bf16[272,256]{1,0:T(8,128)(2,1)S(1)} collective-permute-done((bf16[272,256]{1,0:T(8,128)(2,1)}, bf16[272,256]{1,0:T(8,128)(2,1)S(1)}, u32[]{:S(2)}, u32[]{:S(2)}) %collective-permute-start.2) | collective-permute-done | bytes 139296 | tf_op jit(solution)/shard_map/ppermute | solution.py:283
  28.8 4.5 %collective-permute-start.6 = (bf16[256,256]{1,0:T(8,128)(2,1)}, bf16[256,256]{1,0:T(8,128)(2,1)S(1)}, u32[]{:S(2)}, u32[]{:S(2)}) collective-permute-start(bf16[256,256]{1,0:T(8,128)(2,1)} %get-tuple-element.49), channel_id=1, source_target_pairs={{0,6},{2,4},{4,2},{6,0},{8,14},{10,12},{12,10},{14,8},{1,7},{3,5},... | collective-permute-start | bytes 393224 | tf_op jit(solution)/shard_map/ppermute | solution.py:283
  35.7 3.1 %remote_tiles.1 = (bf16[3,40,64,128]{3,2,1,0:T(8,128)(2,1)S(1)}, bf16[40,64,128]{2,1,0:T(8,128)(2,1)S(1)}) custom-call(bf16[5,64]{1,0:T(8,128)(2,1)S(1)} %concatenate.3.warp_ref, bf16[2,2,64,64]{3,2,1,0:T(8,128)(2,1)S(1)} %copy-done.1, f32[2,2,64,64]{3,2,1,0:T(8,128)S(1)} %copy-done), custom_call_target="tpu_custom_call" | custom-call | flops 128 | bytes 128 | tf_op jit(solution)/shard_map/remote_tiles/pallas_call | solution.py:314
  38.9 2.6 %collective-permute-start.8 = (bf16[256,256]{1,0:T(8,128)(2,1)}, bf16[256,256]{1,0:T(8,128)(2,1)S(1)}, u32[]{:S(2)}, u32[]{:S(2)}) collective-permute-start(bf16[256,256]{1,0:T(8,128)(2,1)} %get-tuple-element.51), channel_id=1, source_target_pairs={{0,10},{2,8},{4,14},{6,12},{8,2},{10,0},{12,6},{14,4},{1,11},{3,9}... | collective-permute-start | bytes 393224 | tf_op jit(solution)/shard_map/ppermute | solution.py:283
  41.4 2.3 %collective-permute-start.9 = (bf16[256,256]{1,0:T(8,128)(2,1)}, bf16[256,256]{1,0:T(8,128)(2,1)S(1)}, u32[]{:S(2)}, u32[]{:S(2)}) collective-permute-start(bf16[256,256]{1,0:T(8,128)(2,1)} %get-tuple-element.52), channel_id=1, source_target_pairs={{0,12},{2,14},{4,8},{6,10},{8,4},{10,6},{12,0},{14,2},{1,13},{3,15... | collective-permute-start | bytes 393224 | tf_op jit(solution)/shard_map/ppermute | solution.py:283
  43.7 2.8 %collective-permute-start.10 = (bf16[256,256]{1,0:T(8,128)(2,1)}, bf16[256,256]{1,0:T(8,128)(2,1)S(1)}, u32[]{:S(2)}, u32[]{:S(2)}) collective-permute-start(bf16[256,256]{1,0:T(8,128)(2,1)} %get-tuple-element.53), channel_id=1, source_target_pairs={{0,14},{2,12},{4,10},{6,8},{8,6},{10,4},{12,2},{14,0},{1,15},{3,13... | collective-permute-start | bytes 393224 | tf_op jit(solution)/shard_map/ppermute | solution.py:283
  46.5 0.9 copy-done.4
  47.4 1.2 %remote_0.1.own = bf16[32,64,256]{2,1,0:T(8,128)(2,1)S(1)} custom-call(bf16[3,40,64,128]{3,2,1,0:T(8,128)(2,1)S(1)} %get-tuple-element.45.tiles, bf16[2,2,64,64]{3,2,1,0:T(8,128)(2,1)S(1)} %copy-done.1, f32[2,2,64,64]{3,2,1,0:T(8,128)S(1)} %copy-done, bf16[272,256]{1,0:T(8,128)(2,1)S(1)} %copy-done.4, bf16[272,256]{1,0:T(8,128)(2,1)S(1)} %collective-permute-done.3.rest_1_, ...), custom_call_target="tpu_custom_call" | custom-call | flops 48 | bytes 48 | tf_op jit(solution)/shard_map/remote_0/pallas_call | solution.py:331
  48.7 4.7 %collective-permute-done.7.rest_4_ = bf16[256,256]{1,0:T(8,128)(2,1)S(1)} collective-permute-done((bf16[256,256]{1,0:T(8,128)(2,1)}, bf16[256,256]{1,0:T(8,128)(2,1)S(1)}, u32[]{:S(2)}, u32[]{:S(2)}) %collective-permute-start.7) | collective-permute-done | bytes 131104 | tf_op jit(solution)/shard_map/ppermute | solution.py:283
  53.5 4.1 %collective-permute-done.8.rest_5_ = bf16[256,256]{1,0:T(8,128)(2,1)S(1)} collective-permute-done((bf16[256,256]{1,0:T(8,128)(2,1)}, bf16[256,256]{1,0:T(8,128)(2,1)S(1)}, u32[]{:S(2)}, u32[]{:S(2)}) %collective-permute-start.8) | collective-permute-done | bytes 131104 | tf_op jit(solution)/shard_map/ppermute | solution.py:283
  57.6 1.4 %remote_1.1.own = bf16[32,64,256]{2,1,0:T(8,128)(2,1)S(1)} custom-call(bf16[3,40,64,128]{3,2,1,0:T(8,128)(2,1)S(1)} %get-tuple-element.45.tiles, bf16[2,2,64,64]{3,2,1,0:T(8,128)(2,1)S(1)} %copy-done.1, f32[2,2,64,64]{3,2,1,0:T(8,128)S(1)} %copy-done, bf16[256,256]{1,0:T(8,128)(2,1)S(1)} %copy-done.5, bf16[256,256]{1,0:T(8,128)(2,1)S(1)} %collective-permute-done.4.rest_1_, ...), custom_call_target="tpu_custom_call" | custom-call | flops 48 | bytes 48 | tf_op jit(solution)/shard_map/remote_1/pallas_call | solution.py:331
  59.7 2.8 %collective-permute-start.23 = (bf16[256,256]{1,0:T(8,128)(2,1)S(1)}, bf16[256,256]{1,0:T(8,128)(2,1)S(1)}, u32[]{:S(2)}, u32[]{:S(2)}) collective-permute-start(bf16[256,256]{1,0:T(8,128)(2,1)S(1)} %get-tuple-element.66), channel_id=1, source_target_pairs={{0,12},{2,14},{4,8},{6,10},{8,4},{10,6},{12,0},{14,2},{1,13},{3,15... | collective-permute-start | bytes 393224 | tf_op jit(solution)/shard_map/ppermute | solution.py:283
  62.6 3.2 %collective-permute-start.24 = (bf16[256,256]{1,0:T(8,128)(2,1)S(1)}, bf16[256,256]{1,0:T(8,128)(2,1)S(1)}, u32[]{:S(2)}, u32[]{:S(2)}) collective-permute-start(bf16[256,256]{1,0:T(8,128)(2,1)S(1)} %get-tuple-element.67), channel_id=1, source_target_pairs={{0,4},{2,6},{4,0},{6,2},{8,12},{10,14},{12,8},{14,10},{1,5},{3,7},... | collective-permute-start | bytes 393224 | tf_op jit(solution)/shard_map/ppermute | solution.py:283
  66.2 4.0 %collective-permute-start.27 = (bf16[256,256]{1,0:T(8,128)(2,1)S(1)}, bf16[256,256]{1,0:T(8,128)(2,1)S(1)}, u32[]{:S(2)}, u32[]{:S(2)}) collective-permute-start(bf16[256,256]{1,0:T(8,128)(2,1)S(1)} %get-tuple-element.70), channel_id=1, source_target_pairs={{0,10},{2,8},{4,14},{6,12},{8,2},{10,0},{12,6},{14,4},{1,11},{3,9}... | collective-permute-start | bytes 393224 | tf_op jit(solution)/shard_map/ppermute | solution.py:283
  70.9 4.4 %collective-permute-start.29 = (bf16[256,256]{1,0:T(8,128)(2,1)S(1)}, bf16[256,256]{1,0:T(8,128)(2,1)S(1)}, u32[]{:S(2)}, u32[]{:S(2)}) collective-permute-start(bf16[256,256]{1,0:T(8,128)(2,1)S(1)} %get-tuple-element.72), channel_id=1, source_target_pairs={{0,14},{2,12},{4,10},{6,8},{8,6},{10,4},{12,2},{14,0},{1,15},{3,13... | collective-permute-start | bytes 393224 | tf_op jit(solution)/shard_map/ppermute | solution.py:283
  75.2 3.6 %collective-permute-done.25.rest_3_ = bf16[256,256]{1,0:T(8,128)(2,1)S(1)} collective-permute-done((bf16[256,256]{1,0:T(8,128)(2,1)S(1)}, bf16[256,256]{1,0:T(8,128)(2,1)S(1)}, u32[]{:S(2)}, u32[]{:S(2)}) %collective-permute-start.25) | collective-permute-done | bytes 131104 | tf_op jit(solution)/shard_map/ppermute | solution.py:283
  78.8 3.3 %collective-permute-start.18 = (bf16[256,256]{1,0:T(8,128)(2,1)S(1)}, bf16[256,256]{1,0:T(8,128)(2,1)S(1)}, u32[]{:S(2)}, u32[]{:S(2)}) collective-permute-start(bf16[256,256]{1,0:T(8,128)(2,1)S(1)} %get-tuple-element.61), channel_id=1, source_target_pairs={{0,12},{2,14},{4,8},{6,10},{8,4},{10,6},{12,0},{14,2},{1,13},{3,15... | collective-permute-start | bytes 393224 | tf_op jit(solution)/shard_map/ppermute | solution.py:283
  82.0 4.9 %collective-permute-done.27.rest_5_ = bf16[256,256]{1,0:T(8,128)(2,1)S(1)} collective-permute-done((bf16[256,256]{1,0:T(8,128)(2,1)S(1)}, bf16[256,256]{1,0:T(8,128)(2,1)S(1)}, u32[]{:S(2)}, u32[]{:S(2)}) %collective-permute-start.27) | collective-permute-done | bytes 131104 | tf_op jit(solution)/shard_map/ppermute | solution.py:283
  87.3 3.8 %collective-permute-start.20 = (bf16[256,256]{1,0:T(8,128)(2,1)S(1)}, bf16[256,256]{1,0:T(8,128)(2,1)S(1)}, u32[]{:S(2)}, u32[]{:S(2)}) collective-permute-start(bf16[256,256]{1,0:T(8,128)(2,1)S(1)} %get-tuple-element.63), channel_id=1, source_target_pairs={{0,8},{2,10},{4,12},{6,14},{8,0},{10,2},{12,4},{14,6},{1,9},{3,11}... | collective-permute-start | bytes 393224 | tf_op jit(solution)/shard_map/ppermute | solution.py:283
  91.3 7.4 %collective-permute-start.16 = (bf16[256,256]{1,0:T(8,128)(2,1)S(1)}, bf16[256,256]{1,0:T(8,128)(2,1)S(1)}, u32[]{:S(2)}, u32[]{:S(2)}) collective-permute-start(bf16[256,256]{1,0:T(8,128)(2,1)S(1)} %get-tuple-element.58), channel_id=1, source_target_pairs={{0,6},{2,4},{4,2},{6,0},{8,14},{10,12},{12,10},{14,8},{1,7},{3,5},... | collective-permute-start | bytes 393224 | tf_op jit(solution)/shard_map/ppermute | solution.py:283
  98.7 4.0 %collective-permute-start.17 = (bf16[256,256]{1,0:T(8,128)(2,1)S(1)}, bf16[256,256]{1,0:T(8,128)(2,1)S(1)}, u32[]{:S(2)}, u32[]{:S(2)}) collective-permute-start(bf16[256,256]{1,0:T(8,128)(2,1)S(1)} %get-tuple-element.59), channel_id=1, source_target_pairs={{0,14},{2,12},{4,10},{6,8},{8,6},{10,4},{12,2},{14,0},{1,15},{3,13... | collective-permute-start | bytes 393224 | tf_op jit(solution)/shard_map/ppermute | solution.py:283
  102.7 1.7 %eval_0.1.rest_5_ = f32[8,8,64,256]{3,2,1,0:T(8,128)} custom-call(bf16[1,64]{1,0:T(2,128)(2,1)S(1)} %bitcast.3, bf16[64,64]{1,0:T(8,128)(2,1)S(1)} %copy-done.3, f32[64,64]{1,0:T(8,128)S(1)} %copy-done.2, bf16[256,256]{1,0:T(8,128)(2,1)S(1)} %get-tuple-element.65.rest_0_, bf16[256,256]{1,0:T(8,128)(2,1)S(1)} %collective-permute-done.23.rest_1_, ...), custom_call_target="tpu_custom_call" | custom-call | flops 8 | bytes 8 | tf_op jit(solution)/shard_map/eval_0/pallas_call | solution.py:365
  104.4 1.4 %eval_1.1.rest_3_ = f32[8,8,64,256]{3,2,1,0:T(8,128)} custom-call(bf16[1,64]{1,0:T(2,128)(2,1)S(1)} %bitcast.4, bf16[64,64]{1,0:T(8,128)(2,1)S(1)} %copy-done.3, f32[64,64]{1,0:T(8,128)S(1)} %copy-done.2, bf16[256,256]{1,0:T(8,128)(2,1)S(1)} %get-tuple-element.60.rest_0_, ...), custom_call_target="tpu_custom_call", output_to_operand_aliasing={{}: (8, {})} | custom-call | flops 5 | bytes 5 | tf_op jit(solution)/shard_map/eval_1/pallas_call | solution.py:365
  105.8 3.4 %collective-permute-done.16.rest_1_ = bf16[256,256]{1,0:T(8,128)(2,1)S(1)} collective-permute-done((bf16[256,256]{1,0:T(8,128)(2,1)S(1)}, bf16[256,256]{1,0:T(8,128)(2,1)S(1)}, u32[]{:S(2)}, u32[]{:S(2)}) %collective-permute-start.16) | collective-permute-done | bytes 131104 | tf_op jit(solution)/shard_map/ppermute | solution.py:283
  109.3 1.2 %eval_2.1 = f32[8,8,64,256]{3,2,1,0:T(8,128)} custom-call(bf16[1,64]{1,0:T(2,128)(2,1)S(1)} %bitcast.5, bf16[64,64]{1,0:T(8,128)(2,1)S(1)} %copy-done.3, f32[64,64]{1,0:T(8,128)S(1)} %copy-done.2, bf16[256,256]{1,0:T(8,128)(2,1)S(1)} %collective-permute-done.15.rest_0_, ...), custom_call_target="tpu_custom_call", output_to_operand_aliasing={{}: (6, {})} | custom-call | flops 3 | bytes 3 | tf_op jit(solution)/shard_map/eval_2/pallas_call | solution.py:365
  (57 shorter events, 6.0 us)
Async XLA Ops:
  8.8 14.5 %collective-permute-start = (bf16[272,256]{1,0:T(8,128)(2,1)}, bf16[272,256]{1,0:T(8,128)(2,1)S(1)}, u32[]{:S(2)}, u32[]{:S(2)}) collective-permute-start(bf16[272,256]{1,0:T(8,128)(2,1)} %get-tuple-element.40), channel_id=1, source_target_pairs={{0,12},{2,14},{4,8},{6,10},{8,4},{10,6},{12,0},{14,2},{1,13},{3,15... | collective-permute-start | bytes 417800 | tf_op jit(solution)/shard_map/ppermute | solution.py:283
  13.9 12.0 %collective-permute-start.1 = (bf16[272,256]{1,0:T(8,128)(2,1)}, bf16[272,256]{1,0:T(8,128)(2,1)S(1)}, u32[]{:S(2)}, u32[]{:S(2)}) collective-permute-start(bf16[272,256]{1,0:T(8,128)(2,1)} %get-tuple-element.41), channel_id=1, source_target_pairs={{0,4},{2,6},{4,0},{6,2},{8,12},{10,14},{12,8},{14,10},{1,5},{3,7},... | collective-permute-start | bytes 417800 | tf_op jit(solution)/shard_map/ppermute | solution.py:283
  13.9 14.9 %collective-permute-start.2 = (bf16[272,256]{1,0:T(8,128)(2,1)}, bf16[272,256]{1,0:T(8,128)(2,1)S(1)}, u32[]{:S(2)}, u32[]{:S(2)}) collective-permute-start(bf16[272,256]{1,0:T(8,128)(2,1)} %get-tuple-element.42), channel_id=1, source_target_pairs={{0,8},{2,10},{4,12},{6,14},{8,0},{10,2},{12,4},{14,6},{1,9},{3,11}... | collective-permute-start | bytes 417800 | tf_op jit(solution)/shard_map/ppermute | solution.py:283
  14.5 6.4 %collective-permute-start.4 = (bf16[256,256]{1,0:T(8,128)(2,1)}, bf16[256,256]{1,0:T(8,128)(2,1)S(1)}, u32[]{:S(2)}, u32[]{:S(2)}) collective-permute-start(bf16[256,256]{1,0:T(8,128)(2,1)} %get-tuple-element.47), channel_id=1, source_target_pairs={{0,2},{2,0},{4,6},{6,4},{8,10},{10,8},{12,14},{14,12},{1,3},{3,1},... | collective-permute-start | bytes 393224 | tf_op jit(solution)/shard_map/ppermute | solution.py:283
  16.2 12.6 %collective-permute-start.3 = (bf16[272,256]{1,0:T(8,128)(2,1)}, bf16[272,256]{1,0:T(8,128)(2,1)S(1)}, u32[]{:S(2)}, u32[]{:S(2)}) collective-permute-start(bf16[272,256]{1,0:T(8,128)(2,1)} %get-tuple-element.43), channel_id=1, source_target_pairs={{0,2},{2,0},{4,6},{6,4},{8,10},{10,8},{12,14},{14,12},{1,3},{3,1},... | collective-permute-start | bytes 417800 | tf_op jit(solution)/shard_map/ppermute | solution.py:283
  20.9 18.0 %collective-permute-start.11 = (bf16[272,256]{1,0:T(8,128)(2,1)}, bf16[272,256]{1,0:T(8,128)(2,1)S(1)}, u32[]{:S(2)}, u32[]{:S(2)}) collective-permute-start(bf16[272,256]{1,0:T(8,128)(2,1)} %get-tuple-element.54), channel_id=1, source_target_pairs={{0,6},{2,4},{4,2},{6,0},{8,14},{10,12},{12,10},{14,8},{1,7},{3,5},... | collective-permute-start | bytes 417800 | tf_op jit(solution)/shard_map/ppermute | solution.py:283
  23.3 18.2 %collective-permute-start.12 = (bf16[272,256]{1,0:T(8,128)(2,1)}, bf16[272,256]{1,0:T(8,128)(2,1)S(1)}, u32[]{:S(2)}, u32[]{:S(2)}) collective-permute-start(bf16[272,256]{1,0:T(8,128)(2,1)} %get-tuple-element.55), channel_id=1, source_target_pairs={{0,10},{2,8},{4,14},{6,12},{8,2},{10,0},{12,6},{14,4},{1,11},{3,9}... | collective-permute-start | bytes 417800 | tf_op jit(solution)/shard_map/ppermute | solution.py:283
  25.8 17.9 %collective-permute-start.13 = (bf16[272,256]{1,0:T(8,128)(2,1)}, bf16[272,256]{1,0:T(8,128)(2,1)S(1)}, u32[]{:S(2)}, u32[]{:S(2)}) collective-permute-start(bf16[272,256]{1,0:T(8,128)(2,1)} %get-tuple-element.56), channel_id=1, source_target_pairs={{0,14},{2,12},{4,10},{6,8},{8,6},{10,4},{12,2},{14,0},{1,15},{3,13... | collective-permute-start | bytes 417800 | tf_op jit(solution)/shard_map/ppermute | solution.py:283
  28.8 10.0 %collective-permute-start.5 = (bf16[256,256]{1,0:T(8,128)(2,1)}, bf16[256,256]{1,0:T(8,128)(2,1)S(1)}, u32[]{:S(2)}, u32[]{:S(2)}) collective-permute-start(bf16[256,256]{1,0:T(8,128)(2,1)} %get-tuple-element.48), channel_id=1, source_target_pairs={{0,4},{2,6},{4,0},{6,2},{8,12},{10,14},{12,8},{14,10},{1,5},{3,7},... | collective-permute-start | bytes 393224 | tf_op jit(solution)/shard_map/ppermute | solution.py:283
  28.8 19.9 %collective-permute-start.6 = (bf16[256,256]{1,0:T(8,128)(2,1)}, bf16[256,256]{1,0:T(8,128)(2,1)S(1)}, u32[]{:S(2)}, u32[]{:S(2)}) collective-permute-start(bf16[256,256]{1,0:T(8,128)(2,1)} %get-tuple-element.49), channel_id=1, source_target_pairs={{0,6},{2,4},{4,2},{6,0},{8,14},{10,12},{12,10},{14,8},{1,7},{3,5},... | collective-permute-start | bytes 393224 | tf_op jit(solution)/shard_map/ppermute | solution.py:283
  38.8 14.7 %collective-permute-start.7 = (bf16[256,256]{1,0:T(8,128)(2,1)}, bf16[256,256]{1,0:T(8,128)(2,1)S(1)}, u32[]{:S(2)}, u32[]{:S(2)}) collective-permute-start(bf16[256,256]{1,0:T(8,128)(2,1)} %get-tuple-element.50), channel_id=1, source_target_pairs={{0,8},{2,10},{4,12},{6,14},{8,0},{10,2},{12,4},{14,6},{1,9},{3,11}... | collective-permute-start | bytes 393224 | tf_op jit(solution)/shard_map/ppermute | solution.py:283
  38.9 18.7 %collective-permute-start.8 = (bf16[256,256]{1,0:T(8,128)(2,1)}, bf16[256,256]{1,0:T(8,128)(2,1)S(1)}, u32[]{:S(2)}, u32[]{:S(2)}) collective-permute-start(bf16[256,256]{1,0:T(8,128)(2,1)} %get-tuple-element.51), channel_id=1, source_target_pairs={{0,10},{2,8},{4,14},{6,12},{8,2},{10,0},{12,6},{14,4},{1,11},{3,9}... | collective-permute-start | bytes 393224 | tf_op jit(solution)/shard_map/ppermute | solution.py:283
  41.4 16.2 %collective-permute-start.9 = (bf16[256,256]{1,0:T(8,128)(2,1)}, bf16[256,256]{1,0:T(8,128)(2,1)S(1)}, u32[]{:S(2)}, u32[]{:S(2)}) collective-permute-start(bf16[256,256]{1,0:T(8,128)(2,1)} %get-tuple-element.52), channel_id=1, source_target_pairs={{0,12},{2,14},{4,8},{6,10},{8,4},{10,6},{12,0},{14,2},{1,13},{3,15... | collective-permute-start | bytes 393224 | tf_op jit(solution)/shard_map/ppermute | solution.py:283
  43.7 13.9 %collective-permute-start.10 = (bf16[256,256]{1,0:T(8,128)(2,1)}, bf16[256,256]{1,0:T(8,128)(2,1)S(1)}, u32[]{:S(2)}, u32[]{:S(2)}) collective-permute-start(bf16[256,256]{1,0:T(8,128)(2,1)} %get-tuple-element.53), channel_id=1, source_target_pairs={{0,14},{2,12},{4,10},{6,8},{8,6},{10,4},{12,2},{14,0},{1,15},{3,13... | collective-permute-start | bytes 393224 | tf_op jit(solution)/shard_map/ppermute | solution.py:283
  48.6 10.5 %collective-permute-start.22 = (bf16[32,64,256]{2,1,0:T(8,128)(2,1)S(1)}, bf16[32,64,256]{2,1,0:T(8,128)(2,1)S(1)}, u32[]{:S(2)}, u32[]{:S(2)}) collective-permute-start(bf16[32,64,256]{2,1,0:T(8,128)(2,1)S(1)} %remote_0.1.own), channel_id=1, source_target_pairs={{0,1},{1,0},{2,3},{3,2},{4,5},{5,4},{6,7},{7,6},{8,9},{9,8},{10,11... | collective-permute-start | bytes 3145736 | tf_op jit(solution)/shard_map/ppermute | solution.py:341
  59.0 43.7 %copy-start.2 = (f32[64,64]{1,0:T(8,128)S(1)}, f32[64,64]{1,0:T(8,128)}, u32[]{:S(2)}) copy-start(f32[64,64]{1,0:T(8,128)} %omega_ref.15) | copy-start | bytes 49156
  59.0 43.7 %copy-start.3 = (bf16[64,64]{1,0:T(8,128)(2,1)S(1)}, bf16[64,64]{1,0:T(8,128)(2,1)}, u32[]{:S(2)}) copy-start(bf16[64,64]{1,0:T(8,128)(2,1)} %interp_ref.15) | copy-start | bytes 24580
  59.0 7.1 %collective-permute-start.14 = (bf16[32,64,256]{2,1,0:T(8,128)(2,1)S(1)}, bf16[32,64,256]{2,1,0:T(8,128)(2,1)S(1)}, u32[]{:S(2)}, u32[]{:S(2)}) collective-permute-start(bf16[32,64,256]{2,1,0:T(8,128)(2,1)S(1)} %remote_1.1.own), channel_id=1, source_target_pairs={{0,1},{1,0},{2,3},{3,2},{4,5},{5,4},{6,7},{7,6},{8,9},{9,8},{10,11... | collective-permute-start | bytes 3145736 | tf_op jit(solution)/shard_map/ppermute | solution.py:341
  59.7 11.0 %collective-permute-start.23 = (bf16[256,256]{1,0:T(8,128)(2,1)S(1)}, bf16[256,256]{1,0:T(8,128)(2,1)S(1)}, u32[]{:S(2)}, u32[]{:S(2)}) collective-permute-start(bf16[256,256]{1,0:T(8,128)(2,1)S(1)} %get-tuple-element.66), channel_id=1, source_target_pairs={{0,12},{2,14},{4,8},{6,10},{8,4},{10,6},{12,0},{14,2},{1,13},{3,15... | collective-permute-start | bytes 393224 | tf_op jit(solution)/shard_map/ppermute | solution.py:283
  62.6 8.3 %collective-permute-start.24 = (bf16[256,256]{1,0:T(8,128)(2,1)S(1)}, bf16[256,256]{1,0:T(8,128)(2,1)S(1)}, u32[]{:S(2)}, u32[]{:S(2)}) collective-permute-start(bf16[256,256]{1,0:T(8,128)(2,1)S(1)} %get-tuple-element.67), channel_id=1, source_target_pairs={{0,4},{2,6},{4,0},{6,2},{8,12},{10,14},{12,8},{14,10},{1,5},{3,7},... | collective-permute-start | bytes 393224 | tf_op jit(solution)/shard_map/ppermute | solution.py:283
  65.8 13.0 %collective-permute-start.25 = (bf16[256,256]{1,0:T(8,128)(2,1)S(1)}, bf16[256,256]{1,0:T(8,128)(2,1)S(1)}, u32[]{:S(2)}, u32[]{:S(2)}) collective-permute-start(bf16[256,256]{1,0:T(8,128)(2,1)S(1)} %get-tuple-element.68), channel_id=1, source_target_pairs={{0,8},{2,10},{4,12},{6,14},{8,0},{10,2},{12,4},{14,6},{1,9},{3,11}... | collective-permute-start | bytes 393224 | tf_op jit(solution)/shard_map/ppermute | solution.py:283
  65.9 16.2 %collective-permute-start.26 = (bf16[256,256]{1,0:T(8,128)(2,1)S(1)}, bf16[256,256]{1,0:T(8,128)(2,1)S(1)}, u32[]{:S(2)}, u32[]{:S(2)}) collective-permute-start(bf16[256,256]{1,0:T(8,128)(2,1)S(1)} %get-tuple-element.69), channel_id=1, source_target_pairs={{0,2},{2,0},{4,6},{6,4},{8,10},{10,8},{12,14},{14,12},{1,3},{3,1},... | collective-permute-start | bytes 393224 | tf_op jit(solution)/shard_map/ppermute | solution.py:283
  66.2 20.8 %collective-permute-start.27 = (bf16[256,256]{1,0:T(8,128)(2,1)S(1)}, bf16[256,256]{1,0:T(8,128)(2,1)S(1)}, u32[]{:S(2)}, u32[]{:S(2)}) collective-permute-start(bf16[256,256]{1,0:T(8,128)(2,1)S(1)} %get-tuple-element.70), channel_id=1, source_target_pairs={{0,10},{2,8},{4,14},{6,12},{8,2},{10,0},{12,6},{14,4},{1,11},{3,9}... | collective-permute-start | bytes 393224 | tf_op jit(solution)/shard_map/ppermute | solution.py:283
  70.8 16.5 %collective-permute-start.28 = (bf16[256,256]{1,0:T(8,128)(2,1)S(1)}, bf16[256,256]{1,0:T(8,128)(2,1)S(1)}, u32[]{:S(2)}, u32[]{:S(2)}) collective-permute-start(bf16[256,256]{1,0:T(8,128)(2,1)S(1)} %get-tuple-element.71), channel_id=1, source_target_pairs={{0,6},{2,4},{4,2},{6,0},{8,14},{10,12},{12,10},{14,8},{1,7},{3,5},... | collective-permute-start | bytes 393224 | tf_op jit(solution)/shard_map/ppermute | solution.py:283
  70.9 20.2 %collective-permute-start.29 = (bf16[256,256]{1,0:T(8,128)(2,1)S(1)}, bf16[256,256]{1,0:T(8,128)(2,1)S(1)}, u32[]{:S(2)}, u32[]{:S(2)}) collective-permute-start(bf16[256,256]{1,0:T(8,128)(2,1)S(1)} %get-tuple-element.72), channel_id=1, source_target_pairs={{0,14},{2,12},{4,10},{6,8},{8,6},{10,4},{12,2},{14,0},{1,15},{3,13... | collective-permute-start | bytes 393224 | tf_op jit(solution)/shard_map/ppermute | solution.py:283
  78.8 12.6 %collective-permute-start.18 = (bf16[256,256]{1,0:T(8,128)(2,1)S(1)}, bf16[256,256]{1,0:T(8,128)(2,1)S(1)}, u32[]{:S(2)}, u32[]{:S(2)}) collective-permute-start(bf16[256,256]{1,0:T(8,128)(2,1)S(1)} %get-tuple-element.61), channel_id=1, source_target_pairs={{0,12},{2,14},{4,8},{6,10},{8,4},{10,6},{12,0},{14,2},{1,13},{3,15... | collective-permute-start | bytes 393224 | tf_op jit(solution)/shard_map/ppermute | solution.py:283
  82.0 16.7 %collective-permute-start.19 = (bf16[256,256]{1,0:T(8,128)(2,1)S(1)}, bf16[256,256]{1,0:T(8,128)(2,1)S(1)}, u32[]{:S(2)}, u32[]{:S(2)}) collective-permute-start(bf16[256,256]{1,0:T(8,128)(2,1)S(1)} %get-tuple-element.62), channel_id=1, source_target_pairs={{0,4},{2,6},{4,0},{6,2},{8,12},{10,14},{12,8},{14,10},{1,5},{3,7},... | collective-permute-start | bytes 393224 | tf_op jit(solution)/shard_map/ppermute | solution.py:283
  86.9 18.9 %collective-permute-start.15 = (bf16[256,256]{1,0:T(8,128)(2,1)S(1)}, bf16[256,256]{1,0:T(8,128)(2,1)S(1)}, u32[]{:S(2)}, u32[]{:S(2)}) collective-permute-start(bf16[256,256]{1,0:T(8,128)(2,1)S(1)} %get-tuple-element.57), channel_id=1, source_target_pairs={{0,10},{2,8},{4,14},{6,12},{8,2},{10,0},{12,6},{14,4},{1,11},{3,9}... | collective-permute-start | bytes 393224 | tf_op jit(solution)/shard_map/ppermute | solution.py:283
  87.3 17.1 %collective-permute-start.20 = (bf16[256,256]{1,0:T(8,128)(2,1)S(1)}, bf16[256,256]{1,0:T(8,128)(2,1)S(1)}, u32[]{:S(2)}, u32[]{:S(2)}) collective-permute-start(bf16[256,256]{1,0:T(8,128)(2,1)S(1)} %get-tuple-element.63), channel_id=1, source_target_pairs={{0,8},{2,10},{4,12},{6,14},{8,0},{10,2},{12,4},{14,6},{1,9},{3,11}... | collective-permute-start | bytes 393224 | tf_op jit(solution)/shard_map/ppermute | solution.py:283
  91.1 13.3 %collective-permute-start.21 = (bf16[256,256]{1,0:T(8,128)(2,1)S(1)}, bf16[256,256]{1,0:T(8,128)(2,1)S(1)}, u32[]{:S(2)}, u32[]{:S(2)}) collective-permute-start(bf16[256,256]{1,0:T(8,128)(2,1)S(1)} %get-tuple-element.64), channel_id=1, source_target_pairs={{0,2},{2,0},{4,6},{6,4},{8,10},{10,8},{12,14},{14,12},{1,3},{3,1},... | collective-permute-start | bytes 393224 | tf_op jit(solution)/shard_map/ppermute | solution.py:283
  91.3 17.9 %collective-permute-start.16 = (bf16[256,256]{1,0:T(8,128)(2,1)S(1)}, bf16[256,256]{1,0:T(8,128)(2,1)S(1)}, u32[]{:S(2)}, u32[]{:S(2)}) collective-permute-start(bf16[256,256]{1,0:T(8,128)(2,1)S(1)} %get-tuple-element.58), channel_id=1, source_target_pairs={{0,6},{2,4},{4,2},{6,0},{8,14},{10,12},{12,10},{14,8},{1,7},{3,5},... | collective-permute-start | bytes 393224 | tf_op jit(solution)/shard_map/ppermute | solution.py:283
  98.7 10.5 %collective-permute-start.17 = (bf16[256,256]{1,0:T(8,128)(2,1)S(1)}, bf16[256,256]{1,0:T(8,128)(2,1)S(1)}, u32[]{:S(2)}, u32[]{:S(2)}) collective-permute-start(bf16[256,256]{1,0:T(8,128)(2,1)S(1)} %get-tuple-element.59), channel_id=1, source_target_pairs={{0,14},{2,12},{4,10},{6,8},{8,6},{10,4},{12,2},{14,0},{1,15},{3,13... | collective-permute-start | bytes 393224 | tf_op jit(solution)/shard_map/ppermute | solution.py:283
  (5 other events, 68.2 us)
